TPU v7x, 32 devices: a whole 2x2x4 slice. The times are simulated.
32 devices in a mesh: dp: 8 (over z, y), mp: 4 (over x, core).
Axes of the slice: x: 2, y: 2, z: 4, core: 2. Of those that a mesh axis runs over, the one named last changes fastest.
Arguments:
- tokens: bfloat16 [256, 5120], P('dp'), may hold values from -14 to 14
- parent_keys: bfloat16 [64, 256, 1024], P('dp', None, 'mp'), may hold values from -56 to 56
- parent_values: bfloat16 [64, 256, 1024], P('dp', None, 'mp'), may hold values from -24 to 24
- parent_blocks: int32 [64], replicated, may hold values from 1 to 2
- child_parent: int32 [256], replicated, may hold values from 0 to 63, as said below
- child_count: int32 [8], P('dp'), may hold values from 24 to 32, as said below
- node_shard: int32 [256], replicated, may hold values from 0 to 7, as said below
- attn_gain: float32 [5120], replicated, may hold values from 0.5 to 1.5
- w_query: bfloat16 [5120, 3072], P(None, 'mp'), may hold values from -1 to 1
- w_key: bfloat16 [5120, 1024], P(None, 'mp'), may hold values from -1 to 1
- w_value: bfloat16 [5120, 1024], P(None, 'mp'), may hold values from -0.078125 to 0.078125
- w_out: bfloat16 [3072, 5120], P('mp'), may hold values from -0.109375 to 0.109375
- reward_up: bfloat16 [8, 5120, 512], P('dp', 'mp'), may hold values from -0.078125 to 0.078125
- reward_out: float32 [8, 512], P('dp'), may hold values from -0.25 to 0.25
Outputs:
- rewards: float32 [8, 384], P(None, 'dp')
Inputs may be any that keep to these rules, and one draw needn't show every extreme that they name: `child_parent`: the children of one index of dp name parents of one index of dp at most 8 times, and exactly 8 times for some pair at every index. `child_count`: every index of dp holds 24 or more live children, and some index holds 32. `node_shard`: the children of one index of dp name one shard at most 6 times, exactly 6 times for some shard at every index.
All inputs are finite; a program needn't handle non-finite values.
Results may differ from a plain program's by a relative error of at most 0.015.
Values may be sent and summed in bfloat16 or wider, within the bound.
No kernel may reach another device: no remote copies, remote signals or barrier semaphores. Data moves between devices by JAX's collectives and lax.ppermute only.
A program may use at most 128 MiB of HBM per device.

v0:
```python
import jax
import jax.numpy as jnp
from jax import lax
from jax.sharding import PartitionSpec as P

D = 5120
HEADS = 24
KVH = 8
HD = 128
STEPS = 8


def slot_ranks(targets, live):
    count = targets.shape[-1]
    index = jnp.arange(count)
    earlier = index[None, :] < index[:, None]
    same = (targets[:, :, None] == targets[:, None, :]) & earlier[None] & live[:, None, :]
    return jnp.sum(same.astype(jnp.int32), -1)


def attend_part(query, keys, values, valid):
    scale = HD ** (-0.5)
    scores = jnp.einsum("ckgd,ctkd->ckgt", query, keys, preferred_element_type=jnp.float32) * scale
    scores = jnp.where(valid[:, None, None, :], scores, -jnp.inf)
    top = jnp.max(scores, -1)
    weight = jnp.exp(scores - top[..., None])
    total = jnp.sum(weight, -1)
    summed = jnp.einsum(
        "ckgt,ctkd->ckgd", weight.astype(jnp.bfloat16), values, preferred_element_type=jnp.float32
    )
    return (top, total, summed)


def normalize(state, gain):
    return (state * lax.rsqrt(jnp.mean(state * state, -1, keepdims=True) + 1e-06) * gain).astype(
        jnp.bfloat16
    )


def shards(
    tokens,
    parent_keys,
    parent_values,
    parent_blocks,
    child_parent,
    child_count,
    node_shard,
    attn_gain,
    w_query,
    w_key,
    w_value,
    w_out,
    reward_up,
    reward_out,
):
    groups = lax.axis_size("dp")
    own = lax.axis_index("dp")
    children = tokens.shape[0]
    width = tokens.shape[1]
    kv_cols = w_key.shape[1]
    kv_heads = kv_cols // HD
    group = HEADS // KVH
    held = parent_keys.shape[0]
    prefix = parent_keys.shape[1]
    capacity = max(2, 2 * children // groups)
    reward_cap = max(2, 3 * children // (2 * groups))
    parents_all = child_parent.reshape(groups, children)
    source_all = parents_all // held
    local_all = parents_all % held
    rank_all = slot_ranks(source_all, jnp.ones(source_all.shape, bool))
    slot_ids = jnp.arange(capacity)
    outgoing = (source_all[:, None, :] == own) & (rank_all[:, None, :] == slot_ids[None, :, None])
    local_parent = jnp.sum(outgoing.astype(jnp.int32) * local_all[:, None, :], -1)
    my_parents = lax.dynamic_index_in_dim(parents_all, own, 0, keepdims=False)
    my_source = lax.dynamic_index_in_dim(source_all, own, 0, keepdims=False)
    my_rank = lax.dynamic_index_in_dim(rank_all, own, 0, keepdims=False)
    positions = jnp.arange(prefix)
    send_keys = parent_keys[local_parent]
    send_values = parent_values[local_parent]
    got_keys, got_values = (
        lax.all_to_all(send_keys, "dp", split_axis=0, concat_axis=0, tiled=True),
        lax.all_to_all(send_values, "dp", split_axis=0, concat_axis=0, tiled=True),
    )
    cache_keys = got_keys[my_source, my_rank].reshape(children, prefix, kv_heads, HD)
    cache_values = got_values[my_source, my_rank].reshape(children, prefix, kv_heads, HD)
    valid = positions[None, :] < (parent_blocks[my_parents] * 128)[:, None]
    slice_width = width // lax.axis_size("mp")
    slice_start = lax.axis_index("mp") * slice_width
    state = tokens.astype(jnp.float32)
    normed = normalize(state, attn_gain)
    new_keys = jnp.zeros((children, STEPS, kv_heads, HD), jnp.bfloat16)
    new_values = jnp.zeros((children, STEPS, kv_heads, HD), jnp.bfloat16)
    step_rows = []
    for step in range(STEPS):
        query = (
            jnp.dot(normed, w_query, preferred_element_type=jnp.float32)
            .astype(jnp.bfloat16)
            .reshape(children, kv_heads, group, HD)
        )
        key_now = (
            jnp.dot(normed, w_key, preferred_element_type=jnp.float32)
            .astype(jnp.bfloat16)
            .reshape(children, kv_heads, HD)
        )
        value_now = (
            jnp.dot(normed, w_value, preferred_element_type=jnp.float32)
            .astype(jnp.bfloat16)
            .reshape(children, kv_heads, HD)
        )
        new_keys = new_keys.at[:, step].set(key_now)
        new_values = new_values.at[:, step].set(value_now)
        top_a, total_a, sum_a = attend_part(query, cache_keys, cache_values, valid)
        recent = jnp.broadcast_to(jnp.arange(STEPS)[None, :] <= step, (children, STEPS))
        top_b, total_b, sum_b = attend_part(query, new_keys, new_values, recent)
        both = jnp.maximum(top_a, top_b)
        fac_a = jnp.exp(top_a - both)
        fac_b = jnp.exp(top_b - both)
        attn = (
            (sum_a * fac_a[..., None] + sum_b * fac_b[..., None])
            / (total_a * fac_a + total_b * fac_b)[..., None]
        ).astype(jnp.bfloat16)
        partial_out = jnp.dot(attn.reshape(children, -1), w_out, preferred_element_type=jnp.float32)
        state = state + lax.psum(partial_out, "mp")
        step_rows.append(
            lax.dynamic_slice_in_dim(state, slice_start, slice_width, 1).astype(jnp.bfloat16)
        )
        if step + 1 < STEPS:
            normed = normalize(state, attn_gain)
    rows_here = jnp.stack(step_rows, 1)
    my_shard = lax.dynamic_index_in_dim(
        node_shard.reshape(groups, children), own, 0, keepdims=False
    )
    live = jnp.arange(children) < child_count[0]
    shard_rank = slot_ranks(my_shard[None], live[None])[0]
    sending = (
        (my_shard[None, None, :] == jnp.arange(groups)[:, None, None])
        & (shard_rank[None, None, :] == jnp.arange(reward_cap)[None, :, None])
        & live[None, None, :]
    )
    outbound = jnp.einsum(
        "dqj,jtx->dqtx", sending.astype(jnp.bfloat16), rows_here, preferred_element_type=jnp.float32
    ).astype(jnp.bfloat16)
    arrived = lax.all_to_all(outbound, "dp", split_axis=0, concat_axis=0, tiled=True)
    flat = arrived.reshape(groups * reward_cap * STEPS, slice_width)
    lifted = jnp.dot(flat, reward_up[0], preferred_element_type=jnp.float32)
    wide = flat.astype(jnp.float32)
    squares = jnp.sum(wide * wide, -1)
    lifted, squares = (
        lax.psum(lifted.astype(jnp.bfloat16), "mp").astype(jnp.float32),
        lax.psum(squares.astype(jnp.bfloat16), "mp").astype(jnp.float32),
    )
    lifted = lifted * lax.rsqrt(squares[:, None] / D + 1e-06)
    values = jnp.sum(jax.nn.silu(lifted) * reward_out[0], -1)
    return values.reshape(groups * reward_cap, STEPS).T


def solution(mesh):
    placed = (
        P("dp", None),
        P("dp", None, "mp"),
        P("dp", None, "mp"),
        P(),
        P(),
        P("dp"),
        P(),
        P(),
        P(None, "mp"),
        P(None, "mp"),
        P(None, "mp"),
        P("mp", None),
        P("dp", "mp", None),
        P("dp", None),
    )
    return jax.shard_map(
        shards, mesh=mesh, in_specs=placed, out_specs=P(None, "dp"), check_vma=False
    )
```

profile of v0, /device:TPU:0, one launch (start us, length us, event | category | flops | bytes accessed | tf_op | source)
XLA Modules:
  0.0 939.6 jit_solution(16886894572992579955)
XLA Ops:
  8.1 6.7 gather_fusion.1
  14.8 7.2 all-to-all-start
  22.0 6.7 gather_fusion.3
  28.6 176.5 %all-to-all-done = bf16[8,8,256,256]{3,2,1,0:T(8,128)(2,1)} async-done(((bf16[8,8,256,256]{3,2,1,0:T(8,128)(2,1)}), bf16[8,8,256,256]{3,2,1,0:T(8,128)(2,1)}, u32[]{:S(2)}, u32[]{:S(2)}) %all-to-all-start) | async-done | bytes 8388640 | tf_op jit(solution)/shard_map/all_to_all | solution.py:81
  205.2 5.1 all-to-all-start.1
  222.5 6.2 gather_fusion.2
  228.6 6.4 copy.125
  239.9 152.6 %all-to-all-done.1 = bf16[8,8,256,256]{3,2,1,0:T(8,128)(2,1)} async-done(((bf16[8,8,256,256]{3,2,1,0:T(8,128)(2,1)}), bf16[8,8,256,256]{3,2,1,0:T(8,128)(2,1)}, u32[]{:S(2)}, u32[]{:S(2)}) %all-to-all-start.1) | async-done | bytes 8388640 | tf_op jit(solution)/shard_map/all_to_all | solution.py:82
  392.5 6.2 gather_fusion.4
  398.6 6.4 copy.127
  408.6 5.6 fusion.207
  415.8 31.3 %all-reduce.12.cloned.1.call-done = f32[32,5120]{1,0:T(8,128)} async-done(((f32[32,5120]{1,0:T(8,128)}), f32[32,5120]{1,0:T(8,128)}) %all-reduce.12.cloned.1.call-update) | async-done | bytes 655376 | tf_op jit(solution)/shard_map/psum | solution.py:123
  463.2 5.6 fusion.208
  469.1 33.7 %all-reduce.14.cloned.1.call-done = f32[32,5120]{1,0:T(8,128)} async-done(((f32[32,5120]{1,0:T(8,128)}), f32[32,5120]{1,0:T(8,128)}) %all-reduce.14.cloned.1.call-update) | async-done | bytes 655376 | tf_op jit(solution)/shard_map/psum | solution.py:123
  523.4 5.6 fusion.209
  529.2 33.7 %all-reduce.16.cloned.1.call-done = f32[32,5120]{1,0:T(8,128)} async-done(((f32[32,5120]{1,0:T(8,128)}), f32[32,5120]{1,0:T(8,128)}) %all-reduce.16.cloned.1.call-update) | async-done | bytes 655376 | tf_op jit(solution)/shard_map/psum | solution.py:123
  583.7 5.6 fusion.210
  590.0 33.3 %all-reduce.18.cloned.1.call-done = f32[32,5120]{1,0:T(8,128)} async-done(((f32[32,5120]{1,0:T(8,128)}), f32[32,5120]{1,0:T(8,128)}) %all-reduce.18.cloned.1.call-update) | async-done | bytes 655376 | tf_op jit(solution)/shard_map/psum | solution.py:123
  625.7 4.8 convolution_convert_fusion.4
  644.0 5.6 fusion.211
  651.1 32.4 %all-reduce.20.cloned.1.call-done = f32[32,5120]{1,0:T(8,128)} async-done(((f32[32,5120]{1,0:T(8,128)}), f32[32,5120]{1,0:T(8,128)}) %all-reduce.20.cloned.1.call-update) | async-done | bytes 655376 | tf_op jit(solution)/shard_map/psum | solution.py:123
  698.8 5.6 fusion.212
  707.7 30.7 %all-reduce.22.cloned.1.call-done = f32[32,5120]{1,0:T(8,128)} async-done(((f32[32,5120]{1,0:T(8,128)}), f32[32,5120]{1,0:T(8,128)}) %all-reduce.22.cloned.1.call-update) | async-done | bytes 655376 | tf_op jit(solution)/shard_map/psum | solution.py:123
  740.0 4.8 convolution_convert_fusion.2
  758.3 5.6 fusion.213
  767.4 30.5 %all-reduce.24.cloned.1.call-done = f32[32,5120]{1,0:T(8,128)} async-done(((f32[32,5120]{1,0:T(8,128)}), f32[32,5120]{1,0:T(8,128)}) %all-reduce.24.cloned.1.call-update) | async-done | bytes 655376 | tf_op jit(solution)/shard_map/psum | solution.py:123
  800.1 4.8 convolution_convert_fusion.1
  825.0 5.6 fusion.214
  832.8 31.7 %all-reduce.26.cloned.1.call-done = f32[32,5120]{1,0:T(8,128)} async-done(((f32[32,5120]{1,0:T(8,128)}), f32[32,5120]{1,0:T(8,128)}) %all-reduce.26.cloned.1.call-update) | async-done | bytes 655376 | tf_op jit(solution)/shard_map/psum | solution.py:123
  867.9 28.9 %all_to_all.15 = bf16[8,6,8,1280]{3,2,1,0:T(8,128)(2,1)S(1)} all-to-all(bf16[8,6,8,1280]{3,2,1,0:T(8,128)(2,1)S(1)} %copy.159), channel_id=1, replica_groups=mesh['dp'=8,'mp'=4] {'dp'}, dimensions={0} | all-to-all | bytes 1966080 | tf_op jit(solution)/shard_map/all_to_all | solution.py:143
  901.0 6.1 psum.79
  907.1 23.3 %all-reduce.28.cloned.1.call-done = bf16[384,512]{1,0:T(8,128)(2,1)} async-done(((bf16[384,512]{1,0:T(8,128)(2,1)}), bf16[384,512]{1,0:T(8,128)(2,1)}) %all-reduce.28.cloned.1.call-update) | async-done | bytes 393232 | tf_op jit(solution)/shard_map/psum | solution.py:149
  (313 shorter events, 169.6 us)
Async XLA Ops:
  6.5 208.8 %copy-start = (bf16[5120,256]{1,0:T(8,128)(2,1)S(1)}, bf16[5120,256]{1,0:T(8,128)(2,1)}, u32[]{:S(2)}) copy-start(bf16[5120,256]{1,0:T(8,128)(2,1)} %param.55) | copy-start | bytes 7864324
  14.8 190.4 %all-to-all-start = ((bf16[8,8,256,256]{3,2,1,0:T(8,128)(2,1)}), bf16[8,8,256,256]{3,2,1,0:T(8,128)(2,1)}, u32[]{:S(2)}, u32[]{:S(2)}) async-start(bf16[8,8,256,256]{3,2,1,0:T(8,128)(2,1)} %bitcast.253), calls=%async_computation | async-start | bytes 16777216 | tf_op jit(solution)/shard_map/all_to_all | solution.py:81
  205.2 5.2 copy-start.9
  205.2 5.4 copy-start.25
  205.2 187.3 %all-to-all-start.1 = ((bf16[8,8,256,256]{3,2,1,0:T(8,128)(2,1)}), bf16[8,8,256,256]{3,2,1,0:T(8,128)(2,1)}, u32[]{:S(2)}, u32[]{:S(2)}) async-start(bf16[8,8,256,256]{3,2,1,0:T(8,128)(2,1)} %bitcast.252), calls=%async_computation.1 | async-start | bytes 16777216 | tf_op jit(solution)/shard_map/all_to_all | solution.py:82
  210.3 236.9 %all-reduce.12.cloned.1.call-start = ((), (), s32[]{:S(2)}) async-start(), calls=%async_computation.3 | async-start | bytes 1310720 | tf_op jit(solution)/shard_map/psum | solution.py:123
  215.3 5.1 copy-start.1
  221.5 7.1 copy-start.39
  398.6 6.4 copy-start.42
  398.6 6.4 copy-start.43
  414.1 88.6 %all-reduce.14.cloned.1.call-start = ((), (), s32[]{:S(2)}) async-start(), calls=%async_computation.4 | async-start | bytes 1310720 | tf_op jit(solution)/shard_map/psum | solution.py:123
  449.4 5.4 copy-start.2
  463.1 39.6 %copy-start.11 = (f32[32,5120]{1,0:T(8,128)S(1)}, f32[32,5120]{1,0:T(8,128)}, u32[]{:S(2)}) copy-start(f32[32,5120]{1,0:T(8,128)} %copy-done.10) | copy-start | bytes 1966084
  468.8 94.1 %all-reduce.16.cloned.1.call-start = ((), (), s32[]{:S(2)}) async-start(), calls=%async_computation.5 | async-start | bytes 1310720 | tf_op jit(solution)/shard_map/psum | solution.py:123
  505.0 5.4 copy-start.3
  529.0 94.3 %all-reduce.18.cloned.1.call-start = ((), (), s32[]{:S(2)}) async-start(), calls=%async_computation.6 | async-start | bytes 1310720 | tf_op jit(solution)/shard_map/psum | solution.py:123
  565.4 5.4 copy-start.4
  570.7 8.9 copy-start.49
  589.3 94.2 %all-reduce.20.cloned.1.call-start = ((), (), s32[]{:S(2)}) async-start(), calls=%async_computation.7 | async-start | bytes 1310720 | tf_op jit(solution)/shard_map/psum | solution.py:123
  625.7 5.4 copy-start.5
  631.1 8.9 copy-start.48
  649.6 88.8 %all-reduce.22.cloned.1.call-start = ((), (), s32[]{:S(2)}) async-start(), calls=%async_computation.8 | async-start | bytes 1310720 | tf_op jit(solution)/shard_map/psum | solution.py:123
  686.0 5.4 copy-start.6
  704.5 93.4 %all-reduce.24.cloned.1.call-start = ((), (), s32[]{:S(2)}) async-start(), calls=%async_computation.9 | async-start | bytes 1310720 | tf_op jit(solution)/shard_map/psum | solution.py:123
  740.0 5.4 copy-start.7
  764.0 100.6 %all-reduce.26.cloned.1.call-start = ((), (), s32[]{:S(2)}) async-start(), calls=%async_computation.10 | async-start | bytes 1310720 | tf_op jit(solution)/shard_map/psum | solution.py:123
  800.1 6.0 copy-start.8
  817.5 4.8 copy-start.30
  825.0 41.3 %copy-start.45 = (pred[6,32]{1,0:T(8,128)(4,1)S(1)}, pred[6,32]{1,0:T(8,128)(4,1)}, u32[]{:S(2)}) copy-start(pred[6,32]{1,0:T(8,128)(4,1)} %iota_compare_fusion.4) | copy-start | bytes 580
  830.6 99.9 %all-reduce.28.cloned.1.call-start = ((), (), s32[]{:S(2)}) async-start(), calls=%async_computation.11 | async-start | bytes 786432 | tf_op jit(solution)/shard_map/psum | solution.py:149
  864.5 33.3 %copy-start.47 = (bf16[1,1280,512]{2,1,0:T(8,128)(2,1)S(1)}, bf16[1,1280,512]{2,1,0:T(8,128)(2,1)}, u32[]{:S(2)}) copy-start(bf16[1,1280,512]{2,1,0:T(8,128)(2,1)} %param.58) | copy-start | bytes 3932164
  867.8 62.7 %copy-start.44 = (f32[1,512]{1,0:T(1,128)S(1)}, f32[1,512]{1,0:T(1,128)}, u32[]{:S(2)}) copy-start(f32[1,512]{1,0:T(1,128)} %param.59) | copy-start | bytes 6148
  (29 other events, 90.0 us)
Sparse Core Ops, SparseCore 0:
  414.3 32.8 all-reduce.11
  468.9 33.7 all-reduce.13
  529.1 33.7 all-reduce.15
  589.4 33.7 all-reduce.17
  649.7 33.7 all-reduce.19
  704.6 33.7 all-reduce.21
  764.1 33.7 all-reduce.23
  830.7 33.7 all-reduce.25
  899.4 31.0 all-reduce.27
where the time goes:
time: 949 us; the launch traced here: 940 us
  waiting for transfers between devices  610 us (64%)
  matrix products  152 us (16%)
  local copies, waits for them, and re-layouts  83.3 us (9%)
  blocking collectives  34.9 us (4%)
  other arithmetic  30.4 us (3%)
  between operations  15.5 us (2%)
  starting transfers between devices  13.8 us (1%)
    psum x8, waiting for transfers between devices, shards(): state = state + lax.psum(partial_out, 'mp')  257 us
    all_to_all x1, waiting for transfers between devices, shards(): lax.all_to_all(send_keys, 'dp', split_axis=0, concat_axis=0, tiled=True)  177 us
    all_to_all x1, waiting for transfers between devices, shards(): lax.all_to_all(send_values, 'dp', split_axis=0, concat_axis=0, tiled=True)  153 us
    dot_general x8, matrix products, shards(): jnp.dot(attn.reshape(children, -1), w_out, preferred_element_type=jnp.flo...  44.7 us
    dot_general x8, matrix products, shards(): jnp.dot(normed, w_query, preferred_element_type=jnp.float32)  38.2 us
    dot_general x16, matrix products, attend_part(): jnp.einsum('ckgd,ctkd->ckgt', query, keys, preferred_element_type=jnp.flo...  33.9 us
    all_to_all x1, blocking collectives, shards(): lax.all_to_all(outbound, 'dp', split_axis=0, concat_axis=0, tiled=True)  28.9 us
    psum x1, waiting for transfers between devices, shards(): lax.psum(lifted.astype(jnp.bfloat16), 'mp').astype(jnp.float32)  23.3 us
  transfers between devices with their start and end apart: 11, of which 11 were waited for; matrix products, arithmetic and copies ran while one was open for 5% of the time, Pallas kernels for 0%

commit v1 on v0

v1 whole, which is shorter than its diff:
```python
import functools

import jax
import jax.numpy as jnp
from jax import lax
from jax.experimental import pallas as pl
from jax.experimental.pallas import tpu as pltpu
from jax.sharding import PartitionSpec as P

D = 5120
HEADS = 24
KVH = 8
HD = 128
STEPS = 8
GROUP = HEADS // KVH
CHUNK = 512
MASKED = -1e30
VMEM = pltpu.VMEM


def slot_ranks(targets, live):
    count = targets.shape[-1]
    index = jnp.arange(count)
    earlier = index[None, :] < index[:, None]
    same = (targets[:, :, None] == targets[:, None, :]) & earlier[None] & live[:, None, :]
    return jnp.sum(same.astype(jnp.int32), -1)


def dot(a, b):
    return jnp.dot(a, b, preferred_element_type=jnp.float32)


def project(attn, w_out, out, first):
    width = out.shape[1]

    @pl.loop(0, width // CHUNK)
    def _(i):
        columns = pl.ds(pl.multiple_of(first + i * CHUNK, CHUNK), CHUNK)
        out[:, pl.ds(pl.multiple_of(i * CHUNK, CHUNK), CHUNK)] = dot(
            attn[...], w_out[:, columns]
        ).astype(out.dtype)


def step_kernel(step, core, own, peer, gain, w_query, w_key, w_value, keys, values, bias, w_out, *rest):
    past_keys, past_values = rest[:step], rest[step : 2 * step]
    part, attn, key_now, value_now, normed, query = rest[2 * step :]
    half = own.shape[1]
    slots = own.shape[0]
    kv_heads = w_key.shape[1] // HD
    first = core[0] == 0
    low = jnp.where(first, own[...], peer[...]).astype(jnp.float32)
    high = jnp.where(first, peer[...], own[...]).astype(jnp.float32)
    squares = jnp.sum(low * low, -1, keepdims=True) + jnp.sum(high * high, -1, keepdims=True)
    factor = lax.rsqrt(squares / D + 1e-06)
    normed[:, :half] = (low * factor * gain[:, :half]).astype(jnp.bfloat16)
    normed[:, half:] = (high * factor * gain[:, half:]).astype(jnp.bfloat16)
    q_cols, kv_cols = w_query.shape[1], w_key.shape[1]
    query[...] = jnp.zeros_like(query)

    @pl.loop(0, D // CHUNK)
    def _(i):
        rows = pl.ds(pl.multiple_of(i * CHUNK, CHUNK), CHUNK)
        block = normed[:, rows]
        query[:, :q_cols] += dot(block, w_query[rows, :])
        query[:, q_cols : q_cols + kv_cols] += dot(block, w_key[rows, :])
        query[:, q_cols + kv_cols :] += dot(block, w_value[rows, :])

    key_now[...] = query[:, q_cols : q_cols + kv_cols].astype(jnp.bfloat16)
    value_now[...] = query[:, q_cols + kv_cols :].astype(jnp.bfloat16)
    recent = slots * (step + 1)
    row = lax.broadcasted_iota(jnp.int32, (GROUP * slots, recent), 0)
    column = lax.broadcasted_iota(jnp.int32, (GROUP * slots, recent), 1)
    same = lax.rem(row, slots) == lax.rem(column, slots)
    for head in range(kv_heads):
        lanes = slice(head * HD, (head + 1) * HD)
        q = jnp.concatenate(
            [query[:, (head * GROUP + g) * HD : (head * GROUP + g + 1) * HD] for g in range(GROUP)], 0
        ).astype(jnp.bfloat16)
        k_new = jnp.concatenate([k[:, lanes] for k in past_keys] + [key_now[:, lanes]], 0)
        v_new = jnp.concatenate([v[:, lanes] for v in past_values] + [value_now[:, lanes]], 0)
        contract = (((1,), (1,)), ((), ()))
        scale = HD ** (-0.5)
        s_old = lax.dot_general(q, keys[:, lanes], contract, preferred_element_type=jnp.float32) * scale
        s_old = s_old + jnp.concatenate([bias[...]] * GROUP, 0)
        s_new = lax.dot_general(q, k_new, contract, preferred_element_type=jnp.float32) * scale
        s_new = jnp.where(same, s_new, MASKED)
        top = jnp.maximum(jnp.max(s_old, -1, keepdims=True), jnp.max(s_new, -1, keepdims=True))
        p_old = jnp.exp(s_old - top)
        p_new = jnp.exp(s_new - top)
        total = jnp.sum(p_old, -1, keepdims=True) + jnp.sum(p_new, -1, keepdims=True)
        summed = dot(p_old.astype(jnp.bfloat16), values[:, lanes]) + dot(p_new.astype(jnp.bfloat16), v_new)
        result = (summed / total).astype(jnp.bfloat16)
        for g in range(GROUP):
            at = (head * GROUP + g) * HD
            attn[:, at : at + HD] = result[g * slots : (g + 1) * slots]
    project(attn, w_out, part, (1 - core[0]) * half)


def expand(step, core, own, peer, gain, w_query, w_key, w_value, keys, values, bias, w_out, past_keys, past_values):
    slots, half = own.shape
    kv_cols = w_key.shape[1]
    q_cols = w_query.shape[1]
    whole = pl.BlockSpec(memory_space=VMEM)
    bf16 = lambda *shape: jax.ShapeDtypeStruct(shape, jnp.bfloat16)
    return pl.pallas_call(
        functools.partial(step_kernel, step),
        out_shape=(bf16(slots, half), bf16(slots, q_cols), bf16(slots, kv_cols), bf16(slots, kv_cols)),
        in_specs=[pl.BlockSpec(memory_space=pltpu.SMEM)] + [whole] * (10 + 2 * step),
        out_specs=[whole] * 4,
        scratch_shapes=[VMEM((slots, D), jnp.bfloat16), VMEM((slots, q_cols + 2 * kv_cols), jnp.float32)],
        compiler_params=pltpu.CompilerParams(vmem_limit_bytes=48 << 20),
        cost_estimate=pl.CostEstimate(
            flops=2 * slots * D * (q_cols + 2 * kv_cols), bytes_accessed=21 << 20, transcendentals=1 << 20
        ),
        name="expand",
    )(core, own, peer, gain, w_query, w_key, w_value, keys, values, bias, w_out, *past_keys, *past_values)


def project_kernel(core, attn, w_out, part):
    project(attn, w_out, part, core[0] * part.shape[1])


def project_own(core, attn, w_out):
    whole = pl.BlockSpec(memory_space=VMEM)
    slots, half = attn.shape[0], w_out.shape[1] // 2
    return pl.pallas_call(
        project_kernel,
        out_shape=jax.ShapeDtypeStruct((slots, half), jnp.float32),
        in_specs=[pl.BlockSpec(memory_space=pltpu.SMEM), whole, whole],
        out_specs=whole,
        compiler_params=pltpu.CompilerParams(vmem_limit_bytes=16 << 20),
        cost_estimate=pl.CostEstimate(
            flops=2 * slots * half * attn.shape[1], bytes_accessed=4 << 20, transcendentals=0
        ),
        name="project_own",
    )(core, attn, w_out)


def shards(
    tokens,
    parent_keys,
    parent_values,
    parent_blocks,
    child_parent,
    child_count,
    node_shard,
    attn_gain,
    w_query,
    w_key,
    w_value,
    w_out,
    reward_up,
    reward_out,
):
    groups = lax.axis_size("dp")
    own = lax.axis_index("dp")
    mp = lax.axis_size("mp")
    me = lax.axis_index("mp")
    core = lax.rem(me, 2)
    core_ref = core.reshape(1).astype(jnp.int32)
    children, width = tokens.shape
    half = width // 2
    held, prefix, kv_cols = parent_keys.shape
    capacity = max(2, 2 * children // groups)
    reward_cap = max(2, 3 * children // (2 * groups))
    slots = groups * capacity
    hidden = reward_out.shape[1] // mp
    swap = [(i, i ^ 1) for i in range(mp)]

    parents_all = child_parent.reshape(groups, children)
    source_all = parents_all // held
    local_all = parents_all % held
    rank_all = slot_ranks(source_all, jnp.ones(source_all.shape, bool))
    slot_ids = jnp.arange(capacity)
    my_source = lax.dynamic_index_in_dim(source_all, own, 0, keepdims=False)
    my_rank = lax.dynamic_index_in_dim(rank_all, own, 0, keepdims=False)
    sending = (my_source[None, None, :] == jnp.arange(groups)[:, None, None]) & (
        my_rank[None, None, :] == slot_ids[None, :, None]
    )
    token_half = lax.dynamic_slice_in_dim(tokens, core * half, half, 1)
    outbound = dot(sending.reshape(slots, children).astype(jnp.bfloat16), token_half).astype(jnp.bfloat16)
    arrived = lax.all_to_all(
        outbound.reshape(groups, capacity, half), "dp", split_axis=0, concat_axis=0, tiled=True
    ).reshape(slots, half)

    taking = (source_all[:, None, :] == own) & (rank_all[:, None, :] == slot_ids[None, :, None])
    pick = lambda table: jnp.sum(jnp.where(taking, table[:, None, :], 0), -1)
    row_parent = pick(local_all).reshape(slots)
    lengths = lax.dynamic_slice_in_dim(parent_blocks, own * held, held, 0) * 128
    valid = jnp.arange(prefix)[None, :] < lengths[:, None]
    usable = (row_parent[:, None, None] == jnp.arange(held)[None, :, None]) & valid[None]
    bias = jnp.where(usable, 0.0, MASKED).astype(jnp.float32).reshape(slots, held * prefix)

    up = reward_up[0].reshape(reward_up.shape[1], mp, hidden)
    pieces = [lax.dynamic_index_in_dim(up, me, 1, keepdims=False)]
    for k in range(1, mp):
        piece = lax.dynamic_index_in_dim(up, lax.rem(me + k, mp), 1, keepdims=False)
        pieces.append(lax.ppermute(piece, "mp", [(i, (i + k) % mp) for i in range(mp)]))
    pieces = jnp.stack(pieces)
    mine = jnp.stack(
        [lax.dynamic_index_in_dim(pieces, lax.rem(me - j + mp, mp), 0, keepdims=False) for j in range(mp)]
    ).reshape(width, hidden)
    up_all = lax.all_gather(mine, "dp", axis=0)
    out_all = lax.all_gather(reward_out[0], "dp", axis=0)
    counts = lax.all_gather(child_count[0], "dp", axis=0)

    keys = parent_keys.reshape(held * prefix, kv_cols)
    values = parent_values.reshape(held * prefix, kv_cols)
    gain = attn_gain.reshape(1, width)
    state = arrived.astype(jnp.float32)
    row_own = arrived
    row_peer = lax.ppermute(row_own, "mp", swap)
    past_keys, past_values, rows_own, rows_peer = [], [], [], []
    for step in range(STEPS):
        part, attn, key_now, value_now = expand(
            step, core_ref, row_own, row_peer, gain, w_query, w_key, w_value, keys, values, bias, w_out,
            past_keys, past_values,
        )
        past_keys.append(key_now)
        past_values.append(value_now)
        from_peer = lax.ppermute(part, "mp", swap)
        chip = project_own(core_ref, attn, w_out) + from_peer.astype(jnp.float32)
        sent = chip.astype(jnp.bfloat16)
        for k in range(2, mp, 2):
            chip = chip + lax.ppermute(sent, "mp", [(i, (i + k) % mp) for i in range(mp)]).astype(jnp.float32)
        state = state + chip
        row_own = state.astype(jnp.bfloat16)
        row_peer = lax.ppermute(row_own, "mp", swap)
        rows_own.append(row_own)
        rows_peer.append(row_peer)

    shard_all = node_shard.reshape(groups, children)
    live_all = jnp.arange(children)[None, :] < counts[:, None]
    reward_rank = slot_ranks(shard_all, live_all)
    row_shard = pick(shard_all).reshape(slots)
    row_rank = pick(reward_rank).reshape(groups, capacity)
    row_live = jnp.any(taking & live_all[:, None, :], -1).reshape(slots)
    flat_own = jnp.concatenate(rows_own, 0)
    flat_peer = jnp.concatenate(rows_peer, 0)
    low = jnp.where(core == 0, flat_own, flat_peer)
    high = jnp.where(core == 0, flat_peer, flat_own)
    flat = jnp.concatenate([low, high], 1)
    wide = flat.astype(jnp.float32)
    squares = jnp.sum(wide * wide, -1, keepdims=True)
    lifted = jnp.einsum("nd,rdh->rnh", flat, up_all, preferred_element_type=jnp.float32)
    chosen = (jnp.tile(row_shard, STEPS)[None, :] == jnp.arange(groups)[:, None])[:, :, None]
    lifted = jnp.sum(jnp.where(chosen, lifted, 0.0), 0) * lax.rsqrt(squares / width + 1e-06)
    out_mine = lax.dynamic_slice_in_dim(out_all, me * hidden, hidden, 1)
    row_out = jnp.sum(jnp.where(chosen, out_mine[:, None, :], 0.0), 0)
    scores = jnp.sum(jax.nn.silu(lifted) * row_out, -1).reshape(STEPS, slots)
    place = (row_shard.reshape(groups, capacity) * groups + jnp.arange(groups)[:, None]) * reward_cap + row_rank
    place = place.reshape(slots)
    put = (place[:, None] == jnp.arange(groups * groups * reward_cap)[None, :]) & row_live[:, None]
    table = jnp.sum(jnp.where(put[None], scores[:, :, None], 0.0), 1)
    table = lax.psum(table, ("dp", "mp"))
    return lax.dynamic_slice_in_dim(table, own * groups * reward_cap, groups * reward_cap, 1)


def solution(mesh):
    placed = (
        P("dp", None),
        P("dp", None, "mp"),
        P("dp", None, "mp"),
        P(),
        P(),
        P("dp"),
        P(),
        P(),
        P(None, "mp"),
        P(None, "mp"),
        P(None, "mp"),
        P("mp", None),
        P("dp", "mp", None),
        P("dp", None),
    )
    return jax.shard_map(
        shards, mesh=mesh, in_specs=placed, out_specs=P(None, "dp"), check_vma=False
    )
```

time: 949 us -> 385 us (0.41)
  waiting for transfers between devices: 610 us -> 74.2 us
  matrix products: 152 us -> 10.4 us
  Pallas kernels: 0 us -> 127 us
  local copies, waits for them, and re-layouts: 83.3 us -> 36.2 us
  blocking collectives: 34.9 us -> 78.5 us
    all_to_all x2 -> x1, waiting for transfers between devices: 329 us -> 6.81 us  [shards(): lax.all_to_all(outbound.reshape(groups, capacity, half), 'dp', split_axis...]
    psum x9 -> x0, waiting for transfers between devices: 281 us -> none  [the longest x8 257 us: shards(): state = state + lax.psum(partial_out, 'mp')]
    dot_general x66 -> x2, matrix products: 152 us -> 10.4 us  [the longest x1 9.48 us: shards(): jnp.einsum('nd,rdh->rnh', flat, up_all, preferred_element_type=jnp.float32)]
    pallas_call x0 -> x16, Pallas kernels: none -> 127 us  [the longest x8 116 us: expand(): pl.pallas_call(functools.partial(step_kernel, step), out_shape=(bf16(slot...]
    ppermute x0 -> x28, waiting for transfers between devices: none -> 67.4 us  [the longest x8 56.1 us: shards(): lax.ppermute(sent, 'mp', [(i, (i + k) % mp) for i in range(mp)])]
    gather x7 -> x0, local copies, waits for them, and re-layouts: 39.2 us -> none  [the longest x2 12.6 us: shards(): got_values[my_source, my_rank].reshape(children, prefix, kv_heads, HD)]
    psum x1, blocking collectives: 6.07 us -> 38.9 us  [shards(): table = lax.psum(table, ('dp', 'mp'))]
    all_to_all x1 -> x0, blocking collectives: 28.9 us -> none  [shards(): lax.all_to_all(outbound, 'dp', split_axis=0, concat_axis=0, tiled=True)]
  transfers between devices with their start and end apart: 11 -> 30, of which waited for: 11 -> 19; matrix products, arithmetic and copies ran while one was open for 5% -> 10% of each run, Pallas kernels for 0% -> 29%
where the time goes in v1:
time: 385 us; the launch traced here: 384 us
  Pallas kernels  127 us (33%)
  blocking collectives  78.5 us (20%)
  waiting for transfers between devices  74.2 us (19%)
  local copies, waits for them, and re-layouts  36.2 us (9%)
  other arithmetic  26.8 us (7%)
  starting transfers between devices  16.6 us (4%)
  between operations  14.7 us (4%)
  matrix products  10.4 us (3%)
    pallas_call x8, Pallas kernels, expand(): pl.pallas_call(functools.partial(step_kernel, step), out_shape=(bf16(slot...  116 us
    ppermute x8, waiting for transfers between devices, shards(): lax.ppermute(sent, 'mp', [(i, (i + k) % mp) for i in range(mp)])  56.1 us
    psum x1, blocking collectives, shards(): table = lax.psum(table, ('dp', 'mp'))  38.9 us
    all_gather x1, blocking collectives, shards(): out_all = lax.all_gather(reward_out[0], 'dp', axis=0)  26.5 us
    unnamed x128, local copies, waits for them, and re-layouts  23.7 us
    unnamed x13, other arithmetic  13.1 us
    unnamed x1, blocking collectives  13.1 us
    ppermute x9, waiting for transfers between devices, shards(): row_peer = lax.ppermute(row_own, 'mp', swap)  10.5 us
  transfers between devices with their start and end apart: 30, of which 19 were waited for; matrix products, arithmetic and copies ran while one was open for 10% of the time, Pallas kernels for 29%

profile of v1, /device:TPU:0, one launch (start us, length us, event | category | flops | bytes accessed | tf_op | source)
XLA Modules:
  0.0 384.2 jit_solution(9620273799618578019)
XLA Ops:
  10.1 13.1 %all-reduce = s32[8]{0:T(128)S(1)} all-reduce(s32[8]{0:T(128)S(1)} %dynamic-update-slice), channel_id=1, replica_groups=mesh['dp'=8,'mp'=4] {'dp'}, use_global_device_ids=true, to_apply=%add | all-reduce | flops 8 | bytes 64
  25.5 3.4 all-to-all-start
  30.8 6.8 %all-to-all-done = bf16[8,8,2560]{2,1,0:T(8,128)(2,1)S(1)} async-done(((bf16[8,8,2560]{2,1,0:T(8,128)(2,1)}), bf16[8,8,2560]{2,1,0:T(8,128)(2,1)S(1)}, u32[]{:S(2)}, u32[]{:S(2)}) %all-to-all-start) | async-done | bytes 327712 | tf_op jit(solution)/shard_map/all_to_all | solution.py:182
  40.1 14.4 %expand.8 = (bf16[64,2560]{1,0:T(8,128)(2,1)S(1)}, bf16[64,768]{1,0:T(8,128)(2,1)S(1)}, bf16[64,256]{1,0:T(8,128)(2,1)S(1)}, bf16[64,256]{1,0:T(8,128)(2,1)S(1)}) custom-call(s32[1]{0:T(128)} %bitcast.15.core, bf16[64,2560]{1,0:T(8,128)(2,1)S(1)} %bitcast.86, bf16[64,2560]{1,0:T(8,128)(2,1)S(1)} %collective-permute-done.3.peer, f32[1,5120]{1,0:T(1,128)S(1)} %bitcast.87, ...), custom_call_target="tpu_custom_call" | custom-call | flops 838860800 | bytes 22020096 | tf_op jit(solution)/shard_map/expand/pallas_call | solution.py:105
  59.1 2.4 copy.42
  61.5 6.2 %collective-permute-done.5 = bf16[64,2560]{1,0:T(8,128)(2,1)} collective-permute-done((bf16[64,2560]{1,0:T(8,128)(2,1)S(1)}, bf16[64,2560]{1,0:T(8,128)(2,1)}, u32[]{:S(2)}, u32[]{:S(2)}) %collective-permute-start.5) | collective-permute-done | bytes 327712 | tf_op jit(solution)/shard_map/ppermute | solution.py:225
  67.7 2.1 constant_dynamic-update-slice_fusion.7
  70.9 1.9 copy.44
  73.3 1.9 copy.45
  76.6 1.9 copy.46
  79.5 14.9 %expand.9 = (bf16[64,2560]{1,0:T(8,128)(2,1)}, bf16[64,768]{1,0:T(8,128)(2,1)S(1)}, bf16[64,256]{1,0:T(8,128)(2,1)S(1)}, bf16[64,256]{1,0:T(8,128)(2,1)S(1)}) custom-call(s32[1]{0:T(128)} %bitcast.15.core, bf16[64,2560]{1,0:T(8,128)(2,1)S(1)} %get-tuple-element.88.own, bf16[64,2560]{1,0:T(8,128)(2,1)} %collective-permute-done.6.peer, ...), custom_call_target="tpu_custom_call" | custom-call | flops 838860800 | bytes 22020096 | tf_op jit(solution)/shard_map/expand/pallas_call | solution.py:105
  97.0 3.2 copy-done.2
  101.6 2.0 fusion.6
  105.5 8.5 %collective-permute-done.8 = bf16[64,2560]{1,0:T(8,128)(2,1)} collective-permute-done((bf16[64,2560]{1,0:T(8,128)(2,1)}, bf16[64,2560]{1,0:T(8,128)(2,1)}, u32[]{:S(2)}, u32[]{:S(2)}) %collective-permute-start.8) | collective-permute-done | bytes 327712 | tf_op jit(solution)/shard_map/ppermute | solution.py:225
  114.0 2.8 constant_dynamic-update-slice_fusion.6
  118.5 14.3 %expand.10 = (bf16[64,2560]{1,0:T(8,128)(2,1)S(1)}, bf16[64,768]{1,0:T(8,128)(2,1)S(1)}, bf16[64,256]{1,0:T(8,128)(2,1)S(1)}, bf16[64,256]{1,0:T(8,128)(2,1)S(1)}) custom-call(s32[1]{0:T(128)} %bitcast.15.core, bf16[64,2560]{1,0:T(8,128)(2,1)S(1)} %get-tuple-element.85.own, bf16[64,2560]{1,0:T(8,128)(2,1)S(1)} %collective-permute-done.9.peer, ...), custom_call_target="tpu_custom_call" | custom-call | flops 838860800 | bytes 22020096 | tf_op jit(solution)/shard_map/expand/pallas_call | solution.py:105
  135.0 9.4 %collective-permute-done.11 = bf16[64,2560]{1,0:T(8,128)(2,1)S(1)} collective-permute-done((bf16[64,2560]{1,0:T(8,128)(2,1)S(1)}, bf16[64,2560]{1,0:T(8,128)(2,1)S(1)}, u32[]{:S(2)}, u32[]{:S(2)}) %collective-permute-start.11) | collective-permute-done | bytes 327712 | tf_op jit(solution)/shard_map/ppermute | solution.py:225
  146.9 14.3 %expand.11 = (bf16[64,2560]{1,0:T(8,128)(2,1)S(1)}, bf16[64,768]{1,0:T(8,128)(2,1)S(1)}, bf16[64,256]{1,0:T(8,128)(2,1)S(1)}, bf16[64,256]{1,0:T(8,128)(2,1)S(1)}) custom-call(s32[1]{0:T(128)} %bitcast.15.core, bf16[64,2560]{1,0:T(8,128)(2,1)S(1)} %get-tuple-element.83.own, bf16[64,2560]{1,0:T(8,128)(2,1)S(1)} %collective-permute-done.12.peer, ...), custom_call_target="tpu_custom_call" | custom-call | flops 838860800 | bytes 22020096 | tf_op jit(solution)/shard_map/expand/pallas_call | solution.py:105
  163.5 9.4 %collective-permute-done.14 = bf16[64,2560]{1,0:T(8,128)(2,1)S(1)} collective-permute-done((bf16[64,2560]{1,0:T(8,128)(2,1)S(1)}, bf16[64,2560]{1,0:T(8,128)(2,1)S(1)}, u32[]{:S(2)}, u32[]{:S(2)}) %collective-permute-start.14) | collective-permute-done | bytes 327712 | tf_op jit(solution)/shard_map/ppermute | solution.py:225
  175.8 14.6 %expand.12 = (bf16[64,2560]{1,0:T(8,128)(2,1)S(1)}, bf16[64,768]{1,0:T(8,128)(2,1)S(1)}, bf16[64,256]{1,0:T(8,128)(2,1)S(1)}, bf16[64,256]{1,0:T(8,128)(2,1)S(1)}) custom-call(s32[1]{0:T(128)} %bitcast.15.core, bf16[64,2560]{1,0:T(8,128)(2,1)S(1)} %get-tuple-element.80.own, bf16[64,2560]{1,0:T(8,128)(2,1)S(1)} %collective-permute-done.15.peer, ...), custom_call_target="tpu_custom_call" | custom-call | flops 838860800 | bytes 22020096 | tf_op jit(solution)/shard_map/expand/pallas_call | solution.py:105
  194.2 26.5 %all-gather = f32[8,1,512]{2,1,0:T(1,128)S(1)} all-gather(f32[1,1,512]{2,1,0:T(1,128)S(1)} %bitcast.106), channel_id=1, replica_groups=mesh['dp'=8,'mp'=4] {'dp'}, dimensions={0}, use_global_device_ids=true | all-gather | bytes 18432 | tf_op jit(solution)/shard_map/all_gather | solution.py:204
  220.7 2.3 constant_dynamic-update-slice_fusion.3
  225.5 14.8 %expand.13 = (bf16[64,2560]{1,0:T(8,128)(2,1)}, bf16[64,768]{1,0:T(8,128)(2,1)S(1)}, bf16[64,256]{1,0:T(8,128)(2,1)S(1)}, bf16[64,256]{1,0:T(8,128)(2,1)S(1)}) custom-call(s32[1]{0:T(128)} %bitcast.15.core, bf16[64,2560]{1,0:T(8,128)(2,1)S(1)} %get-tuple-element.78.own, bf16[64,2560]{1,0:T(8,128)(2,1)S(1)} %collective-permute-done.18.peer, ...), custom_call_target="tpu_custom_call" | custom-call | flops 838860800 | bytes 22020096 | tf_op jit(solution)/shard_map/expand/pallas_call | solution.py:105
  244.7 3.2 copy-done.3
  255.9 7.0 %collective-permute-done.20 = bf16[64,2560]{1,0:T(8,128)(2,1)S(1)} collective-permute-done((bf16[64,2560]{1,0:T(8,128)(2,1)}, bf16[64,2560]{1,0:T(8,128)(2,1)S(1)}, u32[]{:S(2)}, u32[]{:S(2)}) %collective-permute-start.20) | collective-permute-done | bytes 327712 | tf_op jit(solution)/shard_map/ppermute | solution.py:225
  263.0 2.8 constant_dynamic-update-slice_fusion.2
  267.5 14.3 %expand.14 = (bf16[64,2560]{1,0:T(8,128)(2,1)S(1)}, bf16[64,768]{1,0:T(8,128)(2,1)S(1)}, bf16[64,256]{1,0:T(8,128)(2,1)S(1)}, bf16[64,256]{1,0:T(8,128)(2,1)S(1)}) custom-call(s32[1]{0:T(128)} %bitcast.15.core, bf16[64,2560]{1,0:T(8,128)(2,1)S(1)} %get-tuple-element.75.own, bf16[64,2560]{1,0:T(8,128)(2,1)S(1)} %collective-permute-done.21.peer, ...), custom_call_target="tpu_custom_call" | custom-call | flops 838860800 | bytes 22020096 | tf_op jit(solution)/shard_map/expand/pallas_call | solution.py:105
  287.0 7.3 %collective-permute-done.23 = bf16[64,2560]{1,0:T(8,128)(2,1)S(1)} collective-permute-done((bf16[64,2560]{1,0:T(8,128)(2,1)S(1)}, bf16[64,2560]{1,0:T(8,128)(2,1)S(1)}, u32[]{:S(2)}, u32[]{:S(2)}) %collective-permute-start.23) | collective-permute-done | bytes 327712 | tf_op jit(solution)/shard_map/ppermute | solution.py:225
  296.8 14.8 %expand.15 = (bf16[64,2560]{1,0:T(8,128)(2,1)S(1)}, bf16[64,768]{1,0:T(8,128)(2,1)S(1)}, bf16[64,256]{1,0:T(8,128)(2,1)}, bf16[64,256]{1,0:T(8,128)(2,1)}) custom-call(s32[1]{0:T(128)} %bitcast.15.core, bf16[64,2560]{1,0:T(8,128)(2,1)S(1)} %get-tuple-element.73.own, bf16[64,2560]{1,0:T(8,128)(2,1)S(1)} %collective-permute-done.24.peer, ...), custom_call_target="tpu_custom_call" | custom-call | flops 838860800 | bytes 22020096 | tf_op jit(solution)/shard_map/expand/pallas_call | solution.py:105
  315.6 8.4 %collective-permute-done.26 = bf16[64,2560]{1,0:T(8,128)(2,1)S(1)} collective-permute-done((bf16[64,2560]{1,0:T(8,128)(2,1)S(1)}, bf16[64,2560]{1,0:T(8,128)(2,1)S(1)}, u32[]{:S(2)}, u32[]{:S(2)}) %collective-permute-start.26) | collective-permute-done | bytes 327712 | tf_op jit(solution)/shard_map/ppermute | solution.py:225
  327.9 9.5 %select_reduce_fusion.1 = f32[128,512]{1,0:T(8,128)S(1)} fusion(bf16[8,5120,128]{2,1,0:T(8,128)(2,1)} %all-gather.3.cloned.1.call-done, bf16[512,2560]{1,0:T(8,128)(2,1)} %copy-done.33, bf16[512,2560]{1,0:T(8,128)(2,1)S(1)} %get-tuple-element.91, pred[8,512]{1,0:T(8,128)(4,1)S(1)} %iota_compare_fusion.3), kind=kOutput, calls=%fused_computation.9 | convolution fusion | flops 5380177920 | bytes 15994880 | tf_op jit(solution)/shard_map/nd,rdh->rnh/dot_general | solution.py:245
  337.7 38.9 %psum.7 = f32[8,384]{1,0:T(8,128)S(1)} all-reduce(f32[8,384]{1,0:T(8,128)S(1)} %select_reduce_fusion.2), channel_id=1, replica_groups=mesh['dp'=8,'mp'=4] {'dp','mp'}, use_global_device_ids=true, to_apply=%region_11.12 | all-reduce | flops 3072 | bytes 24576 | tf_op jit(solution)/shard_map/psum | solution.py:255
  (248 shorter events, 72.2 us)
Async XLA Ops:
  6.5 32.7 %copy-start.5 = (bf16[8,256,256]{2,1,0:T(8,128)(2,1)S(1)}, bf16[8,256,256]{2,1,0:T(8,128)(2,1)}, u32[]{:S(2)}) copy-start(bf16[8,256,256]{2,1,0:T(8,128)(2,1)} %param.16) | copy-start | bytes 3145732
  25.5 12.0 %all-to-all-start = ((bf16[8,8,2560]{2,1,0:T(8,128)(2,1)}), bf16[8,8,2560]{2,1,0:T(8,128)(2,1)S(1)}, u32[]{:S(2)}, u32[]{:S(2)}) async-start(bf16[8,8,2560]{2,1,0:T(8,128)(2,1)} %fusion.2), calls=%async_computation | async-start | bytes 655360 | tf_op jit(solution)/shard_map/all_to_all | solution.py:182
  29.0 298.9 %all-gather.3.cloned.1.call-start = ((), (), s32[]{:S(2)}) async-start(), calls=%async_computation.1 | async-start | bytes 11796480 | tf_op jit(solution)/shard_map/all_gather | solution.py:203
  37.6 1.6 collective-permute-start.3
  54.4 1.7 collective-permute-start.4
  57.6 10.1 %collective-permute-start.5 = (bf16[64,2560]{1,0:T(8,128)(2,1)S(1)}, bf16[64,2560]{1,0:T(8,128)(2,1)}, u32[]{:S(2)}, u32[]{:S(2)}) collective-permute-start(bf16[64,2560]{1,0:T(8,128)(2,1)S(1)} %fusion.5), channel_id=1, source_target_pairs={{0,2},{1,3},{2,0},{3,1},{4,6},{5,7},{6,4},{7,5},{8,10},{9,11},{10,... | collective-permute-start | bytes 983048 | tf_op jit(solution)/shard_map/ppermute | solution.py:225
  69.8 9.7 %collective-permute-start.6 = (bf16[64,2560]{1,0:T(8,128)(2,1)S(1)}, bf16[64,2560]{1,0:T(8,128)(2,1)}, u32[]{:S(2)}, u32[]{:S(2)}) collective-permute-start(bf16[64,2560]{1,0:T(8,128)(2,1)S(1)} %get-tuple-element.88.own), channel_id=1, source_target_pairs={{0,1},{1,0},{2,3},{3,2},{4,5},{5,4},{6,7},{7,6},{8,9},{9,8},{10,11... | collective-permute-start | bytes 983048 | tf_op jit(solution)/shard_map/ppermute | solution.py:228
  72.8 22.8 %collective-permute-start = (bf16[1280,128]{1,0:T(8,128)(2,1)}, bf16[1280,128]{1,0:T(8,128)(2,1)}, u32[]{:S(2)}, u32[]{:S(2)}) collective-permute-start(bf16[1280,128]{1,0:T(8,128)(2,1)} %bitcast.100), channel_id=1, source_target_pairs={{0,1},{1,2},{2,3},{3,0},{4,5},{5,6},{6,7},{7,4},{8,9},{9,10},{10,1... | collective-permute-start | bytes 983048 | tf_op jit(solution)/shard_map/ppermute | solution.py:198
  75.2 20.5 %collective-permute-start.1 = (bf16[1280,128]{1,0:T(8,128)(2,1)}, bf16[1280,128]{1,0:T(8,128)(2,1)}, u32[]{:S(2)}, u32[]{:S(2)}) collective-permute-start(bf16[1280,128]{1,0:T(8,128)(2,1)} %bitcast.101), channel_id=1, source_target_pairs={{0,2},{1,3},{2,0},{3,1},{4,6},{5,7},{6,4},{7,5},{8,10},{9,11},{10,... | collective-permute-start | bytes 983048 | tf_op jit(solution)/shard_map/ppermute | solution.py:198
  78.5 17.1 %collective-permute-start.2 = (bf16[1280,128]{1,0:T(8,128)(2,1)}, bf16[1280,128]{1,0:T(8,128)(2,1)}, u32[]{:S(2)}, u32[]{:S(2)}) collective-permute-start(bf16[1280,128]{1,0:T(8,128)(2,1)} %bitcast.102), channel_id=1, source_target_pairs={{0,3},{1,0},{2,1},{3,2},{4,7},{5,4},{6,5},{7,6},{8,11},{9,8},{10,9... | collective-permute-start | bytes 983048 | tf_op jit(solution)/shard_map/ppermute | solution.py:198
  94.4 7.1 %collective-permute-start.7 = (bf16[64,2560]{1,0:T(8,128)(2,1)}, bf16[64,2560]{1,0:T(8,128)(2,1)}, u32[]{:S(2)}, u32[]{:S(2)}) collective-permute-start(bf16[64,2560]{1,0:T(8,128)(2,1)} %get-tuple-element.40), channel_id=1, source_target_pairs={{0,1},{1,0},{2,3},{3,2},{4,5},{5,4},{6,7},{7,6},{8,9},{9,8},{10,11... | collective-permute-start | bytes 983048 | tf_op jit(solution)/shard_map/ppermute | solution.py:221
  103.6 10.4 %collective-permute-start.8 = (bf16[64,2560]{1,0:T(8,128)(2,1)}, bf16[64,2560]{1,0:T(8,128)(2,1)}, u32[]{:S(2)}, u32[]{:S(2)}) collective-permute-start(bf16[64,2560]{1,0:T(8,128)(2,1)} %fusion.6), channel_id=1, source_target_pairs={{0,2},{1,3},{2,0},{3,1},{4,6},{5,7},{6,4},{7,5},{8,10},{9,11},{10,... | collective-permute-start | bytes 983048 | tf_op jit(solution)/shard_map/ppermute | solution.py:225
  116.8 1.6 collective-permute-start.9
  132.8 1.7 collective-permute-start.10
  134.5 9.9 %collective-permute-start.11 = (bf16[64,2560]{1,0:T(8,128)(2,1)S(1)}, bf16[64,2560]{1,0:T(8,128)(2,1)S(1)}, u32[]{:S(2)}, u32[]{:S(2)}) collective-permute-start(bf16[64,2560]{1,0:T(8,128)(2,1)S(1)} %fusion.7), channel_id=1, source_target_pairs={{0,2},{1,3},{2,0},{3,1},{4,6},{5,7},{6,4},{7,5},{8,10},{9,11},{10,... | collective-permute-start | bytes 983048 | tf_op jit(solution)/shard_map/ppermute | solution.py:225
  145.3 1.6 collective-permute-start.12
  161.2 1.7 collective-permute-start.13
  163.0 9.9 %collective-permute-start.14 = (bf16[64,2560]{1,0:T(8,128)(2,1)S(1)}, bf16[64,2560]{1,0:T(8,128)(2,1)S(1)}, u32[]{:S(2)}, u32[]{:S(2)}) collective-permute-start(bf16[64,2560]{1,0:T(8,128)(2,1)S(1)} %fusion.8), channel_id=1, source_target_pairs={{0,2},{1,3},{2,0},{3,1},{4,6},{5,7},{6,4},{7,5},{8,10},{9,11},{10,... | collective-permute-start | bytes 983048 | tf_op jit(solution)/shard_map/ppermute | solution.py:225
  174.1 1.6 collective-permute-start.15
  190.4 1.7 collective-permute-start.16
  193.6 27.1 %collective-permute-start.17 = (bf16[64,2560]{1,0:T(8,128)(2,1)}, bf16[64,2560]{1,0:T(8,128)(2,1)S(1)}, u32[]{:S(2)}, u32[]{:S(2)}) collective-permute-start(bf16[64,2560]{1,0:T(8,128)(2,1)} %fusion.9), channel_id=1, source_target_pairs={{0,2},{1,3},{2,0},{3,1},{4,6},{5,7},{6,4},{7,5},{8,10},{9,11},{10,... | collective-permute-start | bytes 983048 | tf_op jit(solution)/shard_map/ppermute | solution.py:225
  223.1 1.6 collective-permute-start.18
  242.2 7.9 %collective-permute-start.19 = (bf16[64,2560]{1,0:T(8,128)(2,1)}, bf16[64,2560]{1,0:T(8,128)(2,1)}, u32[]{:S(2)}, u32[]{:S(2)}) collective-permute-start(bf16[64,2560]{1,0:T(8,128)(2,1)} %get-tuple-element.56), channel_id=1, source_target_pairs={{0,1},{1,0},{2,3},{3,2},{4,5},{5,4},{6,7},{7,6},{8,9},{9,8},{10,11... | collective-permute-start | bytes 983048 | tf_op jit(solution)/shard_map/ppermute | solution.py:221
  252.7 10.2 %collective-permute-start.20 = (bf16[64,2560]{1,0:T(8,128)(2,1)}, bf16[64,2560]{1,0:T(8,128)(2,1)S(1)}, u32[]{:S(2)}, u32[]{:S(2)}) collective-permute-start(bf16[64,2560]{1,0:T(8,128)(2,1)} %fusion.10), channel_id=1, source_target_pairs={{0,2},{1,3},{2,0},{3,1},{4,6},{5,7},{6,4},{7,5},{8,10},{9,11},{10,... | collective-permute-start | bytes 983048 | tf_op jit(solution)/shard_map/ppermute | solution.py:225
  265.7 1.7 collective-permute-start.21
  281.8 2.7 collective-permute-start.22
  284.6 9.7 %collective-permute-start.23 = (bf16[64,2560]{1,0:T(8,128)(2,1)S(1)}, bf16[64,2560]{1,0:T(8,128)(2,1)S(1)}, u32[]{:S(2)}, u32[]{:S(2)}) collective-permute-start(bf16[64,2560]{1,0:T(8,128)(2,1)S(1)} %fusion.11), channel_id=1, source_target_pairs={{0,2},{1,3},{2,0},{3,1},{4,6},{5,7},{6,4},{7,5},{8,10},{9,11},{10,... | collective-permute-start | bytes 983048 | tf_op jit(solution)/shard_map/ppermute | solution.py:225
  295.1 1.6 collective-permute-start.24
  311.6 2.2 collective-permute-start.25
  313.9 10.1 %collective-permute-start.26 = (bf16[64,2560]{1,0:T(8,128)(2,1)S(1)}, bf16[64,2560]{1,0:T(8,128)(2,1)S(1)}, u32[]{:S(2)}, u32[]{:S(2)}) collective-permute-start(bf16[64,2560]{1,0:T(8,128)(2,1)S(1)} %fusion.12), channel_id=1, source_target_pairs={{0,2},{1,3},{2,0},{3,1},{4,6},{5,7},{6,4},{7,5},{8,10},{9,11},{10,... | collective-permute-start | bytes 983048 | tf_op jit(solution)/shard_map/ppermute | solution.py:225
  324.2 1.7 collective-permute-start.27
  327.9 49.4 %copy-start.1 = (bf16[32,5120]{1,0:T(8,128)(2,1)S(1)}, bf16[32,5120]{1,0:T(8,128)(2,1)}, u32[]{:S(2)}) copy-start(bf16[32,5120]{1,0:T(8,128)(2,1)} %param.14) | copy-start | bytes 983044
  (55 other events, 495.2 us)
Sparse Core Ops, SparseCore 0:
  105.6 149.7 all-gather.2

commit v2 on v1

--- a/solution.py
+++ b/solution.py
@@ -24,6 +24,15 @@
     earlier = index[None, :] < index[:, None]
     same = (targets[:, :, None] == targets[:, None, :]) & earlier[None] & live[:, None, :]
     return jnp.sum(same.astype(jnp.int32), -1)
+
+
+def in_parts(x):
+    parts = []
+    for _ in range(3):
+        top = lax.reduce_precision(x, 8, 7)
+        parts.append(top.astype(jnp.bfloat16))
+        x = x - top
+    return jnp.stack(parts)
 
 
 def dot(a, b):
@@ -96,6 +105,10 @@
     project(attn, w_out, part, (1 - core[0]) * half)
 
 
+def held(x):
+    return pltpu.with_memory_space_constraint(x, VMEM)
+
+
 def expand(step, core, own, peer, gain, w_query, w_key, w_value, keys, values, bias, w_out, past_keys, past_values):
     slots, half = own.shape
     kv_cols = w_key.shape[1]
@@ -108,7 +121,7 @@
         in_specs=[pl.BlockSpec(memory_space=pltpu.SMEM)] + [whole] * (10 + 2 * step),
         out_specs=[whole] * 4,
         scratch_shapes=[VMEM((slots, D), jnp.bfloat16), VMEM((slots, q_cols + 2 * kv_cols), jnp.float32)],
-        compiler_params=pltpu.CompilerParams(vmem_limit_bytes=48 << 20),
+        compiler_params=pltpu.CompilerParams(vmem_limit_bytes=20 << 20),
         cost_estimate=pl.CostEstimate(
             flops=2 * slots * D * (q_cols + 2 * kv_cols), bytes_accessed=21 << 20, transcendentals=1 << 20
         ),
@@ -128,7 +141,7 @@
         out_shape=jax.ShapeDtypeStruct((slots, half), jnp.float32),
         in_specs=[pl.BlockSpec(memory_space=pltpu.SMEM), whole, whole],
         out_specs=whole,
-        compiler_params=pltpu.CompilerParams(vmem_limit_bytes=16 << 20),
+        compiler_params=pltpu.CompilerParams(vmem_limit_bytes=8 << 20),
         cost_estimate=pl.CostEstimate(
             flops=2 * slots * half * attn.shape[1], bytes_accessed=4 << 20, transcendentals=0
         ),
@@ -160,7 +173,7 @@
     core_ref = core.reshape(1).astype(jnp.int32)
     children, width = tokens.shape
     half = width // 2
-    held, prefix, kv_cols = parent_keys.shape
+    parents, prefix, kv_cols = parent_keys.shape
     capacity = max(2, 2 * children // groups)
     reward_cap = max(2, 3 * children // (2 * groups))
     slots = groups * capacity
@@ -168,8 +181,8 @@
     swap = [(i, i ^ 1) for i in range(mp)]
 
     parents_all = child_parent.reshape(groups, children)
-    source_all = parents_all // held
-    local_all = parents_all % held
+    source_all = parents_all // parents
+    local_all = parents_all % parents
     rank_all = slot_ranks(source_all, jnp.ones(source_all.shape, bool))
     slot_ids = jnp.arange(capacity)
     my_source = lax.dynamic_index_in_dim(source_all, own, 0, keepdims=False)
@@ -177,36 +190,41 @@
     sending = (my_source[None, None, :] == jnp.arange(groups)[:, None, None]) & (
         my_rank[None, None, :] == slot_ids[None, :, None]
     )
+    my_shard = lax.dynamic_index_in_dim(node_shard.reshape(groups, children), own, 0, keepdims=False)
+    live = jnp.arange(children) < child_count[0]
+    my_reward_rank = slot_ranks(my_shard[None], live[None])[0]
+    notes = jnp.stack([live, my_reward_rank], 1).astype(jnp.bfloat16)
     token_half = lax.dynamic_slice_in_dim(tokens, core * half, half, 1)
-    outbound = dot(sending.reshape(slots, children).astype(jnp.bfloat16), token_half).astype(jnp.bfloat16)
-    arrived = lax.all_to_all(
-        outbound.reshape(groups, capacity, half), "dp", split_axis=0, concat_axis=0, tiled=True
-    ).reshape(slots, half)
+    rows_out = jnp.concatenate([token_half, notes], 1)
+    outbound = dot(sending.reshape(slots, children).astype(jnp.bfloat16), rows_out).astype(jnp.bfloat16)
+    outbound = outbound.reshape(groups, capacity, half + 2)
+    scales = in_parts(reward_out[0]).reshape(capacity, -1)
+    scales = jnp.broadcast_to(scales[None], (groups, *scales.shape))
+    spare = -(scales.shape[2] + 2) % 128
+    outbound = jnp.pad(jnp.concatenate([outbound, scales], 2), ((0, 0), (0, 0), (0, spare)))
+    arrived = lax.all_to_all(outbound, "dp", split_axis=0, concat_axis=0, tiled=True)
+    row_live = (arrived[:, :, half] > 0.5).reshape(slots)
+    row_rank = arrived[:, :, half + 1].astype(jnp.int32)
+    out_all = arrived[:, :, half + 2 : half + 2 + scales.shape[2]].reshape(groups, 3, -1)
+    out_all = jnp.sum(out_all.astype(jnp.float32), 1)
+    arrived = arrived[:, :, :half].reshape(slots, half)
 
     taking = (source_all[:, None, :] == own) & (rank_all[:, None, :] == slot_ids[None, :, None])
     pick = lambda table: jnp.sum(jnp.where(taking, table[:, None, :], 0), -1)
     row_parent = pick(local_all).reshape(slots)
-    lengths = lax.dynamic_slice_in_dim(parent_blocks, own * held, held, 0) * 128
+    lengths = lax.dynamic_slice_in_dim(parent_blocks, own * parents, parents, 0) * 128
     valid = jnp.arange(prefix)[None, :] < lengths[:, None]
-    usable = (row_parent[:, None, None] == jnp.arange(held)[None, :, None]) & valid[None]
-    bias = jnp.where(usable, 0.0, MASKED).astype(jnp.float32).reshape(slots, held * prefix)
-
-    up = reward_up[0].reshape(reward_up.shape[1], mp, hidden)
-    pieces = [lax.dynamic_index_in_dim(up, me, 1, keepdims=False)]
-    for k in range(1, mp):
-        piece = lax.dynamic_index_in_dim(up, lax.rem(me + k, mp), 1, keepdims=False)
-        pieces.append(lax.ppermute(piece, "mp", [(i, (i + k) % mp) for i in range(mp)]))
-    pieces = jnp.stack(pieces)
-    mine = jnp.stack(
-        [lax.dynamic_index_in_dim(pieces, lax.rem(me - j + mp, mp), 0, keepdims=False) for j in range(mp)]
-    ).reshape(width, hidden)
-    up_all = lax.all_gather(mine, "dp", axis=0)
-    out_all = lax.all_gather(reward_out[0], "dp", axis=0)
-    counts = lax.all_gather(child_count[0], "dp", axis=0)
-
-    keys = parent_keys.reshape(held * prefix, kv_cols)
-    values = parent_values.reshape(held * prefix, kv_cols)
+    usable = (row_parent[:, None, None] == jnp.arange(parents)[None, :, None]) & valid[None]
+    bias = jnp.where(usable, 0.0, MASKED).astype(jnp.float32).reshape(slots, parents * prefix)
+
+    up = jnp.transpose(reward_up[0].reshape(reward_up.shape[1], mp, hidden), (1, 0, 2))
+    up = lax.all_to_all(up, "mp", split_axis=0, concat_axis=0, tiled=True).reshape(width, hidden)
+    up_all = lax.all_gather(up, "dp", axis=0)
+
+    keys = held(parent_keys.reshape(parents * prefix, kv_cols))
+    values = held(parent_values.reshape(parents * prefix, kv_cols))
     gain = attn_gain.reshape(1, width)
+    w_query, w_key, w_value, w_out = held(w_query), held(w_key), held(w_value), held(w_out)
     state = arrived.astype(jnp.float32)
     row_own = arrived
     row_peer = lax.ppermute(row_own, "mp", swap)
@@ -229,12 +247,7 @@
         rows_own.append(row_own)
         rows_peer.append(row_peer)
 
-    shard_all = node_shard.reshape(groups, children)
-    live_all = jnp.arange(children)[None, :] < counts[:, None]
-    reward_rank = slot_ranks(shard_all, live_all)
-    row_shard = pick(shard_all).reshape(slots)
-    row_rank = pick(reward_rank).reshape(groups, capacity)
-    row_live = jnp.any(taking & live_all[:, None, :], -1).reshape(slots)
+    row_shard = pick(node_shard.reshape(groups, children)).reshape(slots)
     flat_own = jnp.concatenate(rows_own, 0)
     flat_peer = jnp.concatenate(rows_peer, 0)
     low = jnp.where(core == 0, flat_own, flat_peer)
@@ -252,8 +265,12 @@
     place = place.reshape(slots)
     put = (place[:, None] == jnp.arange(groups * groups * reward_cap)[None, :]) & row_live[:, None]
     table = jnp.sum(jnp.where(put[None], scores[:, :, None], 0.0), 1)
-    table = lax.psum(table, ("dp", "mp"))
-    return lax.dynamic_slice_in_dim(table, own * groups * reward_cap, groups * reward_cap, 1)
+    table = table + lax.ppermute(table, "mp", swap)
+    total = table
+    for k in range(2, mp, 2):
+        total = total + lax.ppermute(table, "mp", [(i, (i + k) % mp) for i in range(mp)])
+    total = jnp.transpose(total.reshape(STEPS, groups, groups * reward_cap), (1, 0, 2))
+    return jnp.sum(lax.all_to_all(total, "dp", split_axis=0, concat_axis=0, tiled=True), 0)
 
 
 def solution(mesh):

time: 385 us -> 318 us (0.83)
  blocking collectives: 78.5 us -> 10.1 us
  Pallas kernels: 127 us -> 69.5 us
  waiting for transfers between devices: 74.2 us -> 102 us
  local copies, waits for them, and re-layouts: 36.2 us -> 61.6 us
  starting transfers between devices: 16.6 us -> 21.3 us
    pallas_call x8, Pallas kernels: 116 us -> 58.9 us  [expand(): pl.pallas_call(functools.partial(step_kernel, step), out_shape=(bf16(slot...]
    psum x1 -> x0, blocking collectives: 38.9 us -> none  [shards(): table = lax.psum(table, ('dp', 'mp'))]
    all_gather x1 -> x0, blocking collectives: 26.5 us -> none  [shards(): out_all = lax.all_gather(reward_out[0], 'dp', axis=0)]
    unnamed x128 -> x184, local copies, waits for them, and re-layouts: 23.7 us -> 48.9 us
    unnamed x1 -> x0, blocking collectives: 13.1 us -> none
    all_to_all x1 -> x2, waiting for transfers between devices: 6.81 us -> 18.1 us  [the longest x1 9.44 us: shards(): lax.all_to_all(outbound, 'dp', split_axis=0, concat_axis=0, tiled=True)]
    ppermute x8, waiting for transfers between devices: 56.1 us -> 67.3 us  [shards(): lax.ppermute(sent, 'mp', [(i, (i + k) % mp) for i in range(mp)])]
    all_to_all x0 -> x1, blocking collectives: none -> 10.1 us  [shards(): lax.all_to_all(total, 'dp', split_axis=0, concat_axis=0, tiled=True)]
  transfers between devices with their start and end apart: 30 -> 30, of which waited for: 19 -> 24; matrix products, arithmetic and copies ran while one was open for 10% -> 10% of each run, Pallas kernels for 29% -> 17%
where the time goes in v2:
time: 318 us; the launch traced here: 316 us
  waiting for transfers between devices  102 us (32%)
  Pallas kernels  69.5 us (22%)
  local copies, waits for them, and re-layouts  61.6 us (19%)
  other arithmetic  25.6 us (8%)
  starting transfers between devices  21.3 us (7%)
  between operations  15.1 us (5%)
  matrix products  10.6 us (3%)
  blocking collectives  10.1 us (3%)
    ppermute x8, waiting for transfers between devices, shards(): lax.ppermute(sent, 'mp', [(i, (i + k) % mp) for i in range(mp)])  67.3 us
    pallas_call x8, Pallas kernels, expand(): pl.pallas_call(functools.partial(step_kernel, step), out_shape=(bf16(slot...  58.9 us
    unnamed x184, local copies, waits for them, and re-layouts  48.9 us
    ppermute x9, waiting for transfers between devices, shards(): row_peer = lax.ppermute(row_own, 'mp', swap)  11.2 us
    pallas_call x8, Pallas kernels, project_own(): pl.pallas_call(project_kernel, out_shape=jax.ShapeDtypeStruct((slots, hal...  10.6 us
    dot_general x1, matrix products, shards(): jnp.einsum('nd,rdh->rnh', flat, up_all, preferred_element_type=jnp.float32)  10.4 us
    all_to_all x1, blocking collectives, shards(): lax.all_to_all(total, 'dp', split_axis=0, concat_axis=0, tiled=True)  10.1 us
    all_to_all x1, waiting for transfers between devices, shards(): lax.all_to_all(outbound, 'dp', split_axis=0, concat_axis=0, tiled=True)  9.44 us
  transfers between devices with their start and end apart: 30, of which 24 were waited for; matrix products, arithmetic and copies ran while one was open for 10% of the time, Pallas kernels for 17%

profile of v2, /device:TPU:0, one launch (start us, length us, event | category | flops | bytes accessed | tf_op | source)
XLA Modules:
  0.0 315.7 jit_solution(9715360875270458951)
XLA Ops:
  11.5 7.3 %all-to-all-start = ((bf16[8,8,2816]{2,1,0:T(8,128)(2,1)}), bf16[8,8,2816]{2,1,0:T(8,128)(2,1)S(1)}, u32[]{:S(2)}, u32[]{:S(2)}) async-start(bf16[8,8,2816]{2,1,0:T(8,128)(2,1)} %fusion.16), calls=%async_computation | async-start | bytes 720896 | tf_op jit(solution)/shard_map/all_to_all | solution.py:205
  20.4 9.4 %all-to-all-done = bf16[8,8,2816]{2,1,0:T(8,128)(2,1)S(1)} async-done(((bf16[8,8,2816]{2,1,0:T(8,128)(2,1)}), bf16[8,8,2816]{2,1,0:T(8,128)(2,1)S(1)}, u32[]{:S(2)}, u32[]{:S(2)}) %all-to-all-start) | async-done | bytes 360480 | tf_op jit(solution)/shard_map/all_to_all | solution.py:205
  31.6 3.2 %copy-done.2 = bf16[768,5120]{1,0:T(8,128)(2,1)S(1)} copy-done((bf16[768,5120]{1,0:T(8,128)(2,1)S(1)}, bf16[768,5120]{1,0:T(8,128)(2,1)}, u32[]{:S(2)}) %copy-start.2) | copy-done | bytes 7864344
  34.8 3.2 %copy-done.7 = bf16[5120,768]{1,0:T(8,128)(2,1)S(1)} copy-done((bf16[5120,768]{1,0:T(8,128)(2,1)S(1)}, bf16[5120,768]{1,0:T(8,128)(2,1)}, u32[]{:S(2)}) %copy-start.7) | copy-done | bytes 7864344
  43.0 7.0 %expand.8 = (bf16[64,2560]{1,0:T(8,128)(2,1)S(1)}, bf16[64,768]{1,0:T(8,128)(2,1)S(1)}, bf16[64,256]{1,0:T(8,128)(2,1)S(1)}, bf16[64,256]{1,0:T(8,128)(2,1)S(1)}) custom-call(s32[1]{0:T(128)} %bitcast.8.core, bf16[64,2560]{1,0:T(8,128)(2,1)S(1)} %slice_bitcast_fusion.own, bf16[64,2560]{1,0:T(8,128)(2,1)S(1)} %collective-permute-done.peer, ...), custom_call_target="tpu_custom_call" | custom-call | flops 838860800 | bytes 22020096 | tf_op jit(solution)/shard_map/expand/pallas_call | solution.py:118
  53.2 8.4 %collective-permute-done.2 = bf16[64,2560]{1,0:T(8,128)(2,1)S(1)} collective-permute-done((bf16[64,2560]{1,0:T(8,128)(2,1)S(1)}, bf16[64,2560]{1,0:T(8,128)(2,1)S(1)}, u32[]{:S(2)}, u32[]{:S(2)}) %collective-permute-start.2) | collective-permute-done | bytes 327712 | tf_op jit(solution)/shard_map/ppermute | solution.py:243
  64.1 7.7 %expand.9 = (bf16[64,2560]{1,0:T(8,128)(2,1)}, bf16[64,768]{1,0:T(8,128)(2,1)S(1)}, bf16[64,256]{1,0:T(8,128)(2,1)S(1)}, bf16[64,256]{1,0:T(8,128)(2,1)S(1)}) custom-call(s32[1]{0:T(128)} %bitcast.8.core, bf16[64,2560]{1,0:T(8,128)(2,1)S(1)} %get-tuple-element.85.own, bf16[64,2560]{1,0:T(8,128)(2,1)S(1)} %collective-permute-done.3.peer, ...), custom_call_target="tpu_custom_call" | custom-call | flops 838860800 | bytes 22020096 | tf_op jit(solution)/shard_map/expand/pallas_call | solution.py:118
  73.8 3.6 %reshape_squeeze.3 = bf16[1280,4,128]{2,1,0:T(4,128)(2,1)} reshape(bf16[1,1280,512]{2,1,0:T(8,128)(2,1)} %param.26) | data formatting | bytes 2621440 | tf_op jit(solution)/shard_map/reshape;squeeze | solution.py:220
  79.9 4.3 %all-to-all-start.1 = ((bf16[4,1280,128]{2,1,0:T(8,128)(2,1)}), bf16[4,1280,128]{2,1,0:T(8,128)(2,1)}, u32[]{:S(2)}, u32[]{:S(2)}) async-start(bf16[4,1280,128]{2,1,0:T(8,128)(2,1)} %bitcast.74), calls=%async_computation.1 | async-start | bytes 2621440 | tf_op jit(solution)/shard_map/all_to_all | solution.py:221
  84.5 3.2 %copy-done.4 = bf16[768,5120]{1,0:T(8,128)(2,1)S(1)} copy-done((bf16[768,5120]{1,0:T(8,128)(2,1)S(1)}, bf16[768,5120]{1,0:T(8,128)(2,1)}, u32[]{:S(2)}) %copy-start.4) | copy-done | bytes 7864344
  93.4 8.7 %all-to-all-done.1 = bf16[4,1280,128]{2,1,0:T(8,128)(2,1)} async-done(((bf16[4,1280,128]{2,1,0:T(8,128)(2,1)}), bf16[4,1280,128]{2,1,0:T(8,128)(2,1)}, u32[]{:S(2)}, u32[]{:S(2)}) %all-to-all-start.1) | async-done | bytes 1310752 | tf_op jit(solution)/shard_map/all_to_all | solution.py:221
  102.1 6.5 %collective-permute-done.5 = bf16[64,2560]{1,0:T(8,128)(2,1)} collective-permute-done((bf16[64,2560]{1,0:T(8,128)(2,1)}, bf16[64,2560]{1,0:T(8,128)(2,1)}, u32[]{:S(2)}, u32[]{:S(2)}) %collective-permute-start.5) | collective-permute-done | bytes 327712 | tf_op jit(solution)/shard_map/ppermute | solution.py:243
  108.6 2.9 constant_dynamic-update-slice_fusion.6
  113.2 3.3 %copy-done.5 = bf16[768,5120]{1,0:T(8,128)(2,1)S(1)} copy-done((bf16[768,5120]{1,0:T(8,128)(2,1)S(1)}, bf16[768,5120]{1,0:T(8,128)(2,1)}, u32[]{:S(2)}) %copy-start.5) | copy-done | bytes 7864344
  116.5 3.3 %copy-done.9 = bf16[5120,768]{1,0:T(8,128)(2,1)S(1)} copy-done((bf16[5120,768]{1,0:T(8,128)(2,1)S(1)}, bf16[5120,768]{1,0:T(8,128)(2,1)}, u32[]{:S(2)}) %copy-start.9) | copy-done | bytes 7864344
  121.0 7.0 %expand.10 = (bf16[64,2560]{1,0:T(8,128)(2,1)S(1)}, bf16[64,768]{1,0:T(8,128)(2,1)S(1)}, bf16[64,256]{1,0:T(8,128)(2,1)S(1)}, bf16[64,256]{1,0:T(8,128)(2,1)S(1)}) custom-call(s32[1]{0:T(128)} %bitcast.8.core, bf16[64,2560]{1,0:T(8,128)(2,1)S(1)} %get-tuple-element.82.own, bf16[64,2560]{1,0:T(8,128)(2,1)S(1)} %collective-permute-done.6.peer, ...), custom_call_target="tpu_custom_call" | custom-call | flops 838860800 | bytes 22020096 | tf_op jit(solution)/shard_map/expand/pallas_call | solution.py:118
  130.4 9.3 %collective-permute-done.8 = bf16[64,2560]{1,0:T(8,128)(2,1)S(1)} collective-permute-done((bf16[64,2560]{1,0:T(8,128)(2,1)S(1)}, bf16[64,2560]{1,0:T(8,128)(2,1)S(1)}, u32[]{:S(2)}, u32[]{:S(2)}) %collective-permute-start.8) | collective-permute-done | bytes 327712 | tf_op jit(solution)/shard_map/ppermute | solution.py:243
  142.2 7.1 %expand.11 = (bf16[64,2560]{1,0:T(8,128)(2,1)S(1)}, bf16[64,768]{1,0:T(8,128)(2,1)S(1)}, bf16[64,256]{1,0:T(8,128)(2,1)S(1)}, bf16[64,256]{1,0:T(8,128)(2,1)S(1)}) custom-call(s32[1]{0:T(128)} %bitcast.8.core, bf16[64,2560]{1,0:T(8,128)(2,1)S(1)} %get-tuple-element.80.own, bf16[64,2560]{1,0:T(8,128)(2,1)S(1)} %collective-permute-done.9.peer, ...), custom_call_target="tpu_custom_call" | custom-call | flops 838860800 | bytes 22020096 | tf_op jit(solution)/shard_map/expand/pallas_call | solution.py:118
  151.6 9.3 %collective-permute-done.11 = bf16[64,2560]{1,0:T(8,128)(2,1)S(1)} collective-permute-done((bf16[64,2560]{1,0:T(8,128)(2,1)S(1)}, bf16[64,2560]{1,0:T(8,128)(2,1)S(1)}, u32[]{:S(2)}, u32[]{:S(2)}) %collective-permute-start.11) | collective-permute-done | bytes 327712 | tf_op jit(solution)/shard_map/ppermute | solution.py:243
  163.8 7.1 %expand.12 = (bf16[64,2560]{1,0:T(8,128)(2,1)S(1)}, bf16[64,768]{1,0:T(8,128)(2,1)S(1)}, bf16[64,256]{1,0:T(8,128)(2,1)S(1)}, bf16[64,256]{1,0:T(8,128)(2,1)S(1)}) custom-call(s32[1]{0:T(128)} %bitcast.8.core, bf16[64,2560]{1,0:T(8,128)(2,1)S(1)} %get-tuple-element.77.own, bf16[64,2560]{1,0:T(8,128)(2,1)S(1)} %collective-permute-done.12.peer, ...), custom_call_target="tpu_custom_call" | custom-call | flops 838860800 | bytes 22020096 | tf_op jit(solution)/shard_map/expand/pallas_call | solution.py:118
  176.7 7.8 %collective-permute-done.14 = bf16[64,2560]{1,0:T(8,128)(2,1)S(1)} collective-permute-done((bf16[64,2560]{1,0:T(8,128)(2,1)}, bf16[64,2560]{1,0:T(8,128)(2,1)S(1)}, u32[]{:S(2)}, u32[]{:S(2)}) %collective-permute-start.14) | collective-permute-done | bytes 327712 | tf_op jit(solution)/shard_map/ppermute | solution.py:243
  194.6 3.2 %copy-done.6 = bf16[768,5120]{1,0:T(8,128)(2,1)S(1)} copy-done((bf16[768,5120]{1,0:T(8,128)(2,1)S(1)}, bf16[768,5120]{1,0:T(8,128)(2,1)}, u32[]{:S(2)}) %copy-start.6) | copy-done | bytes 7864344
  197.9 3.2 %copy-done.10 = bf16[5120,768]{1,0:T(8,128)(2,1)S(1)} copy-done((bf16[5120,768]{1,0:T(8,128)(2,1)S(1)}, bf16[5120,768]{1,0:T(8,128)(2,1)}, u32[]{:S(2)}) %copy-start.10) | copy-done | bytes 7864344
  212.1 8.3 %expand.13 = (bf16[64,2560]{1,0:T(8,128)(2,1)S(1)}, bf16[64,768]{1,0:T(8,128)(2,1)S(1)}, bf16[64,256]{1,0:T(8,128)(2,1)S(1)}, bf16[64,256]{1,0:T(8,128)(2,1)S(1)}) custom-call(s32[1]{0:T(128)} %bitcast.8.core, bf16[64,2560]{1,0:T(8,128)(2,1)S(1)} %get-tuple-element.75.own, bf16[64,2560]{1,0:T(8,128)(2,1)} %collective-permute-done.15.peer, ...), custom_call_target="tpu_custom_call" | custom-call | flops 838860800 | bytes 22020096 | tf_op jit(solution)/shard_map/expand/pallas_call | solution.py:118
  225.1 7.2 %collective-permute-done.17 = bf16[64,2560]{1,0:T(8,128)(2,1)S(1)} collective-permute-done((bf16[64,2560]{1,0:T(8,128)(2,1)S(1)}, bf16[64,2560]{1,0:T(8,128)(2,1)S(1)}, u32[]{:S(2)}, u32[]{:S(2)}) %collective-permute-start.17) | collective-permute-done | bytes 327712 | tf_op jit(solution)/shard_map/ppermute | solution.py:243
  234.4 7.2 %expand.14 = (bf16[64,2560]{1,0:T(8,128)(2,1)S(1)}, bf16[64,768]{1,0:T(8,128)(2,1)S(1)}, bf16[64,256]{1,0:T(8,128)(2,1)S(1)}, bf16[64,256]{1,0:T(8,128)(2,1)S(1)}) custom-call(s32[1]{0:T(128)} %bitcast.8.core, bf16[64,2560]{1,0:T(8,128)(2,1)S(1)} %get-tuple-element.72.own, bf16[64,2560]{1,0:T(8,128)(2,1)S(1)} %collective-permute-done.18.peer, ...), custom_call_target="tpu_custom_call" | custom-call | flops 838860800 | bytes 22020096 | tf_op jit(solution)/shard_map/expand/pallas_call | solution.py:118
  243.9 9.4 %collective-permute-done.20 = bf16[64,2560]{1,0:T(8,128)(2,1)S(1)} collective-permute-done((bf16[64,2560]{1,0:T(8,128)(2,1)S(1)}, bf16[64,2560]{1,0:T(8,128)(2,1)S(1)}, u32[]{:S(2)}, u32[]{:S(2)}) %collective-permute-start.20) | collective-permute-done | bytes 327712 | tf_op jit(solution)/shard_map/ppermute | solution.py:243
  255.2 7.6 %expand.15 = (bf16[64,2560]{1,0:T(8,128)(2,1)S(1)}, bf16[64,768]{1,0:T(8,128)(2,1)S(1)}, bf16[64,256]{1,0:T(8,128)(2,1)}, bf16[64,256]{1,0:T(8,128)(2,1)}) custom-call(s32[1]{0:T(128)} %bitcast.8.core, bf16[64,2560]{1,0:T(8,128)(2,1)S(1)} %get-tuple-element.70.own, bf16[64,2560]{1,0:T(8,128)(2,1)S(1)} %collective-permute-done.21.peer, ...), custom_call_target="tpu_custom_call" | custom-call | flops 838860800 | bytes 22020096 | tf_op jit(solution)/shard_map/expand/pallas_call | solution.py:118
  266.2 9.5 %collective-permute-done.23 = bf16[64,2560]{1,0:T(8,128)(2,1)S(1)} collective-permute-done((bf16[64,2560]{1,0:T(8,128)(2,1)S(1)}, bf16[64,2560]{1,0:T(8,128)(2,1)S(1)}, u32[]{:S(2)}, u32[]{:S(2)}) %collective-permute-start.23) | collective-permute-done | bytes 327712 | tf_op jit(solution)/shard_map/ppermute | solution.py:243
  280.8 10.4 %fusion.3 = f32[512,128]{1,0:T(8,128)S(1)} fusion(bf16[8,5120,128]{2,1,0:T(8,128)(2,1)} %all-gather.2.cloned.1.call-done, bf16[512,2560]{1,0:T(8,128)(2,1)} %copy-done.65, bf16[512,2560]{1,0:T(8,128)(2,1)S(1)} %get-tuple-element.88, pred[8,512]{1,0:T(8,128)(4,1)S(1)} %copy-done.79), kind=kOutput, calls=%fused_computation.9 | convolution fusion | flops 5380177920 | bytes 15994880 | tf_op jit(solution)/shard_map/nd,rdh->rnh/dot_general | solution.py:258
  293.5 3.2 %collective-permute-done.26 = f32[8,384]{1,0:T(8,128)S(1)} collective-permute-done((f32[8,384]{1,0:T(8,128)S(1)}, f32[8,384]{1,0:T(8,128)S(1)}, u32[]{:S(2)}, u32[]{:S(2)}) %collective-permute-start.26) | collective-permute-done | bytes 12320 | tf_op jit(solution)/shard_map/ppermute | solution.py:271
  296.9 10.1 %all_to_all.15 = f32[8,1,384]{2,1,0:T(1,128)S(1)} all-to-all(f32[8,1,384]{2,1,0:T(1,128)S(1)} %reshape.459), channel_id=1, replica_groups=mesh['dp'=8,'mp'=4] {'dp'}, dimensions={0} | all-to-all | bytes 24576 | tf_op jit(solution)/shard_map/all_to_all | solution.py:273
  (312 shorter events, 91.8 us)
Async XLA Ops:
  11.5 18.3 %all-to-all-start = ((bf16[8,8,2816]{2,1,0:T(8,128)(2,1)}), bf16[8,8,2816]{2,1,0:T(8,128)(2,1)S(1)}, u32[]{:S(2)}, u32[]{:S(2)}) async-start(bf16[8,8,2816]{2,1,0:T(8,128)(2,1)} %fusion.16), calls=%async_computation | async-start | bytes 720896 | tf_op jit(solution)/shard_map/all_to_all | solution.py:205
  29.9 1.7 collective-permute-start
  49.9 1.7 collective-permute-start.1
  51.7 9.9 %collective-permute-start.2 = (bf16[64,2560]{1,0:T(8,128)(2,1)S(1)}, bf16[64,2560]{1,0:T(8,128)(2,1)S(1)}, u32[]{:S(2)}, u32[]{:S(2)}) collective-permute-start(bf16[64,2560]{1,0:T(8,128)(2,1)S(1)} %fusion.8), channel_id=1, source_target_pairs={{0,2},{1,3},{2,0},{3,1},{4,6},{5,7},{6,4},{7,5},{8,10},{9,11},{10,... | collective-permute-start | bytes 983048 | tf_op jit(solution)/shard_map/ppermute | solution.py:243
  62.5 1.6 collective-permute-start.3
  73.7 15.4 %collective-permute-start.4 = (bf16[64,2560]{1,0:T(8,128)(2,1)}, bf16[64,2560]{1,0:T(8,128)(2,1)}, u32[]{:S(2)}, u32[]{:S(2)}) collective-permute-start(bf16[64,2560]{1,0:T(8,128)(2,1)} %get-tuple-element.40), channel_id=1, source_target_pairs={{0,1},{1,0},{2,3},{3,2},{4,5},{5,4},{6,7},{7,6},{8,9},{9,8},{10,11... | collective-permute-start | bytes 983048 | tf_op jit(solution)/shard_map/ppermute | solution.py:239
  79.9 22.1 %all-to-all-start.1 = ((bf16[4,1280,128]{2,1,0:T(8,128)(2,1)}), bf16[4,1280,128]{2,1,0:T(8,128)(2,1)}, u32[]{:S(2)}, u32[]{:S(2)}) async-start(bf16[4,1280,128]{2,1,0:T(8,128)(2,1)} %bitcast.74), calls=%async_computation.1 | async-start | bytes 2621440 | tf_op jit(solution)/shard_map/all_to_all | solution.py:221
  84.3 196.5 %all-gather.2.cloned.1.call-start = ((), (), s32[]{:S(2)}) async-start(), calls=%async_computation.3 | async-start | bytes 11796480 | tf_op jit(solution)/shard_map/all_gather | solution.py:222
  91.6 17.0 %collective-permute-start.5 = (bf16[64,2560]{1,0:T(8,128)(2,1)}, bf16[64,2560]{1,0:T(8,128)(2,1)}, u32[]{:S(2)}, u32[]{:S(2)}) collective-permute-start(bf16[64,2560]{1,0:T(8,128)(2,1)} %fusion.9), channel_id=1, source_target_pairs={{0,2},{1,3},{2,0},{3,1},{4,6},{5,7},{6,4},{7,5},{8,10},{9,11},{10,... | collective-permute-start | bytes 983048 | tf_op jit(solution)/shard_map/ppermute | solution.py:243
  111.5 1.6 collective-permute-start.6
  128.0 35.8 %copy-start.45 = (bf16[64,256]{1,0:T(8,128)(2,1)}, bf16[64,256]{1,0:T(8,128)(2,1)S(1)}, u32[]{:S(2)}) copy-start(bf16[64,256]{1,0:T(8,128)(2,1)S(1)} %get-tuple-element.45.rest_2_) | copy-start | bytes 98308
  128.0 35.8 %copy-start.48 = (bf16[64,256]{1,0:T(8,128)(2,1)}, bf16[64,256]{1,0:T(8,128)(2,1)S(1)}, u32[]{:S(2)}) copy-start(bf16[64,256]{1,0:T(8,128)(2,1)S(1)} %get-tuple-element.46.rest_5_.rest_6_.rest_7_.rest_8_.rest_9_) | copy-start | bytes 98308
  128.0 1.7 collective-permute-start.7
  129.8 9.9 %collective-permute-start.8 = (bf16[64,2560]{1,0:T(8,128)(2,1)S(1)}, bf16[64,2560]{1,0:T(8,128)(2,1)S(1)}, u32[]{:S(2)}, u32[]{:S(2)}) collective-permute-start(bf16[64,2560]{1,0:T(8,128)(2,1)S(1)} %fusion.10), channel_id=1, source_target_pairs={{0,2},{1,3},{2,0},{3,1},{4,6},{5,7},{6,4},{7,5},{8,10},{9,11},{10,... | collective-permute-start | bytes 983048 | tf_op jit(solution)/shard_map/ppermute | solution.py:243
  140.6 1.6 collective-permute-start.9
  149.3 1.7 collective-permute-start.10
  151.0 9.9 %collective-permute-start.11 = (bf16[64,2560]{1,0:T(8,128)(2,1)S(1)}, bf16[64,2560]{1,0:T(8,128)(2,1)S(1)}, u32[]{:S(2)}, u32[]{:S(2)}) collective-permute-start(bf16[64,2560]{1,0:T(8,128)(2,1)S(1)} %fusion.11), channel_id=1, source_target_pairs={{0,2},{1,3},{2,0},{3,1},{4,6},{5,7},{6,4},{7,5},{8,10},{9,11},{10,... | collective-permute-start | bytes 983048 | tf_op jit(solution)/shard_map/ppermute | solution.py:243
  162.2 1.6 collective-permute-start.12
  171.0 1.7 collective-permute-start.13
  174.2 10.3 %collective-permute-start.14 = (bf16[64,2560]{1,0:T(8,128)(2,1)}, bf16[64,2560]{1,0:T(8,128)(2,1)S(1)}, u32[]{:S(2)}, u32[]{:S(2)}) collective-permute-start(bf16[64,2560]{1,0:T(8,128)(2,1)} %fusion.12), channel_id=1, source_target_pairs={{0,2},{1,3},{2,0},{3,1},{4,6},{5,7},{6,4},{7,5},{8,10},{9,11},{10,... | collective-permute-start | bytes 983048 | tf_op jit(solution)/shard_map/ppermute | solution.py:243
  187.5 7.1 %collective-permute-start.15 = (bf16[64,2560]{1,0:T(8,128)(2,1)S(1)}, bf16[64,2560]{1,0:T(8,128)(2,1)}, u32[]{:S(2)}, u32[]{:S(2)}) collective-permute-start(bf16[64,2560]{1,0:T(8,128)(2,1)S(1)} %get-tuple-element.75.own), channel_id=1, source_target_pairs={{0,1},{1,0},{2,3},{3,2},{4,5},{5,4},{6,7},{7,6},{8,9},{9,8},{10,11... | collective-permute-start | bytes 983048 | tf_op jit(solution)/shard_map/ppermute | solution.py:246
  220.4 2.0 collective-permute-start.16
  222.4 9.9 %collective-permute-start.17 = (bf16[64,2560]{1,0:T(8,128)(2,1)S(1)}, bf16[64,2560]{1,0:T(8,128)(2,1)S(1)}, u32[]{:S(2)}, u32[]{:S(2)}) collective-permute-start(bf16[64,2560]{1,0:T(8,128)(2,1)S(1)} %fusion.13), channel_id=1, source_target_pairs={{0,2},{1,3},{2,0},{3,1},{4,6},{5,7},{6,4},{7,5},{8,10},{9,11},{10,... | collective-permute-start | bytes 983048 | tf_op jit(solution)/shard_map/ppermute | solution.py:243
  232.7 1.7 collective-permute-start.18
  241.5 1.7 collective-permute-start.19
  243.3 10.0 %collective-permute-start.20 = (bf16[64,2560]{1,0:T(8,128)(2,1)S(1)}, bf16[64,2560]{1,0:T(8,128)(2,1)S(1)}, u32[]{:S(2)}, u32[]{:S(2)}) collective-permute-start(bf16[64,2560]{1,0:T(8,128)(2,1)S(1)} %fusion.14), channel_id=1, source_target_pairs={{0,2},{1,3},{2,0},{3,1},{4,6},{5,7},{6,4},{7,5},{8,10},{9,11},{10,... | collective-permute-start | bytes 983048 | tf_op jit(solution)/shard_map/ppermute | solution.py:243
  253.4 1.7 collective-permute-start.21
  262.8 2.7 collective-permute-start.22
  265.6 10.1 %collective-permute-start.23 = (bf16[64,2560]{1,0:T(8,128)(2,1)S(1)}, bf16[64,2560]{1,0:T(8,128)(2,1)S(1)}, u32[]{:S(2)}, u32[]{:S(2)}) collective-permute-start(bf16[64,2560]{1,0:T(8,128)(2,1)S(1)} %fusion.15), channel_id=1, source_target_pairs={{0,2},{1,3},{2,0},{3,1},{4,6},{5,7},{6,4},{7,5},{8,10},{9,11},{10,... | collective-permute-start | bytes 983048 | tf_op jit(solution)/shard_map/ppermute | solution.py:243
  276.0 1.7 collective-permute-start.24
  291.7 1.2 collective-permute-start.25
  293.0 3.7 %collective-permute-start.26 = (f32[8,384]{1,0:T(8,128)S(1)}, f32[8,384]{1,0:T(8,128)S(1)}, u32[]{:S(2)}, u32[]{:S(2)}) collective-permute-start(f32[8,384]{1,0:T(8,128)S(1)} %add.189), channel_id=1, source_target_pairs={{0,2},{1,3},{2,0},{3,1},{4,6},{5,7},{6,4},{7,5},{8,10},{9,11},{10,... | collective-permute-start | bytes 36872 | tf_op jit(solution)/shard_map/ppermute | solution.py:271
  (84 other events, 585.8 us)
Sparse Core Ops, SparseCore 0:
  102.2 148.9 all-gather.1
